TPU v7x, 32 devices: a whole 2x2x4 slice. The times are simulated.
32 devices in a mesh: scan: 2 (over x), row: 16 (over z, y, core).
Axes of the slice: x: 2, y: 2, z: 4, core: 2. Of those that a mesh axis runs over, the one named last changes fastest.
Arguments:
- object_field: float32 [4, 2, 3072, 384], P('scan', None, 'row'), parts along dimension 0, may hold values from -2.5 to 2.5
- probe: float32 [4, 256, 256], P('scan'), parts along dimension 0, may hold values from -4 to 4
- intensity: float32 [64, 256, 256], P(('scan', 'row')), parts along dimension 0, may hold values from 0 to 3
- row_offset: int32 [64], P(('scan', 'row')), parts along dimension 0, may hold values from 0 to 64
- col_offset: int32 [64], P(('scan', 'row')), parts along dimension 0, may hold values from 0 to 128
- slice_first: int32 [64], P(('scan', 'row')), parts along dimension 0, may hold values from 0 to 1
Outputs:
- object_out: float32 [4, 2, 3072, 384], P('scan', None, 'row'), parts along dimension 0
- probe_out: float32 [4, 256, 256], P('scan'), parts along dimension 0
- misfit_mean: float32 [4], P('scan'), parts along dimension 0
There are 2 independent parts, one for each index of `scan`. A program takes and returns all parts, laid end to end along the dimension named above; each array names one. Nothing has to cross between parts.
All inputs are finite; a program needn't handle non-finite values.
Results may differ from a plain program's by a relative error of at most 0.0003.
Values sent between devices are 32-bit elements; how exact they have to be, the bound alone decides.
A program may use at most 128 MiB of HBM per device.

v0:
```python
import jax
import jax.numpy as jnp
from jax import lax
from jax.sharding import PartitionSpec as P

MARGIN = 64
ITERS = 2


SMOOTHING = 0.01
OBJECT_RATE = 0.25
PROBE_RATE = 0.5
PROPAGATION = 4.0
DAMPING = 1.0
TINY = 1e-06


def padded(shard, sides, width):
    for axis, dim in sides:
        devices, length = (lax.axis_size(axis), shard.shape[dim])
        up = [(i, (i + 1) % devices) for i in range(devices - 1)]
        down = [(j, i) for i, j in up]
        last = lax.slice_in_dim(shard, length - width, length, axis=dim)
        initial = lax.slice_in_dim(shard, 0, width, axis=dim)
        before = lax.ppermute(last, axis, up)
        after = lax.ppermute(initial, axis, down)
        shard = jnp.concatenate([before, shard, after], axis=dim)
    return shard


def dft_tables(length):
    counter = jnp.arange(length, dtype=jnp.int32)
    products = counter[:, None] * counter[None, :] % length
    angular = 2.0 * jnp.pi / length * products.astype(jnp.float32)
    scaling = 1.0 / jnp.sqrt(jnp.float32(length))
    table_re = jnp.cos(angular) * scaling
    table_im = -jnp.sin(angular) * scaling
    signed = (
        jnp.where(counter < length // 2, counter, counter - length).astype(jnp.float32) / length
    )
    phases = -jnp.pi * PROPAGATION * (signed[:, None] ** 2 + signed[None, :] ** 2)
    return (table_re, table_im, jnp.cos(phases), jnp.sin(phases))


def matmul(left, right):
    return jnp.dot(left, right, precision=lax.Precision.HIGHEST, preferred_element_type=jnp.float32)


def complex_times(first_re, first_im, second_re, second_im):
    return (
        first_re * second_re - first_im * second_im,
        first_re * second_im + first_im * second_re,
    )


def transform(field_re, field_im, table_re, table_im):
    left_re = matmul(table_re, field_re) - matmul(table_im, field_im)
    left_im = matmul(table_re, field_im) + matmul(table_im, field_re)
    result_re = matmul(left_re, table_re) - matmul(left_im, table_im)
    result_im = matmul(left_re, table_im) + matmul(left_im, table_re)
    return (result_re, result_im)


def make_objective(intensity, row_offset, col_offset, slice_first, tables):
    table_re, table_im, kernel_re, kernel_im = tables
    length = table_re.shape[0]
    anchor = jnp.zeros((), jnp.int32)

    def objective(extended, probe_now):
        total = jnp.zeros((), jnp.float32)
        weight = jnp.zeros((1, length, length), jnp.float32)
        for index in range(intensity.shape[0]):
            patch = lax.dynamic_slice(
                extended,
                (anchor, anchor, row_offset[index], col_offset[index]),
                (2, 2, length, length),
            )
            chosen = slice_first[index] == 0
            front = jnp.where(chosen, patch[0], patch[1])
            behind = jnp.where(chosen, patch[1], patch[0])
            wave_re, wave_im = complex_times(probe_now[0], probe_now[1], front[0], front[1])
            spec_re, spec_im = transform(wave_re, wave_im, table_re, table_im)
            spec_re, spec_im = complex_times(spec_re, spec_im, kernel_re, kernel_im)
            near_re, near_im = transform(spec_re, spec_im, table_re, -table_im)
            exit_re, exit_im = complex_times(near_re, near_im, behind[0], behind[1])
            far_re, far_im = transform(exit_re, exit_im, table_re, table_im)
            modulus = jnp.sqrt(far_re * far_re + far_im * far_im + SMOOTHING)
            misfit = modulus - jnp.sqrt(intensity[index] + SMOOTHING)
            total = total + jnp.sum(misfit * misfit)
            weight = weight + (front[0] * front[0] + front[1] * front[1])[None]
        return (total, weight)

    return objective


def evaluate(objective, extended, probe_now):
    total, pullback, weight = jax.vjp(objective, extended, probe_now, has_aux=True)
    grad_ext, grad_probe = pullback(jnp.ones_like(total))
    return (grad_ext, grad_probe, weight, total)


def object_rate(probe_now):
    return OBJECT_RATE / (
        jnp.mean(probe_now[0] * probe_now[0] + probe_now[1] * probe_now[1]) + TINY
    )


def renew_probe(probe_now, grad_probe, weight, total):
    grad_sum, weight_sum, total_sum = lax.psum((grad_probe, weight, total), "row")
    renewed = probe_now - PROBE_RATE * grad_sum / (weight_sum + DAMPING)
    return (renewed, total_sum)


def shards(object_field, probe, intensity, row_offset, col_offset, slice_first):
    tables = dft_tables(probe.shape[1])
    objective = make_objective(intensity, row_offset, col_offset, slice_first, tables)
    tile = object_field.shape[2]
    devices = lax.axis_size("row")
    count = intensity.shape[0] * devices * probe.shape[1] * probe.shape[2]
    losses = []
    current = probe
    field = object_field
    for step in range(ITERS):
        extended = padded(field, (("row", 2),), MARGIN)
        grad_ext, grad_probe, weight, total = evaluate(objective, extended, current)
        rate = object_rate(current)
        current, total_sum = renew_probe(current, grad_probe, weight, total)
        losses.append(total_sum / count)
        rims = padded(grad_ext, (("row", 2),), MARGIN)
        height = grad_ext.shape[2]
        owned = grad_ext[:, :, MARGIN : MARGIN + tile]
        owned = owned.at[:, :, :MARGIN].add(rims[:, :, :MARGIN])
        owned = owned.at[:, :, tile - MARGIN :].add(rims[:, :, height + MARGIN :])
        field = field - rate * owned
    return (field, current, jnp.stack(losses))


def solution(mesh):
    placed = (
        P("scan", None, "row", None),
        P("scan", None, None),
        P(("scan", "row"), None, None),
        P(("scan", "row")),
        P(("scan", "row")),
        P(("scan", "row")),
    )
    return jax.shard_map(
        shards,
        mesh=mesh,
        in_specs=placed,
        out_specs=(P("scan", None, "row", None), P("scan", None, None), P("scan")),
        check_vma=False,
    )
```

profile of v0, /device:TPU:1, one launch (start us, length us, event | category | flops | bytes accessed | tf_op | source)
XLA Modules:
  0.0 650.5 jit_solution(15103853979662605747)
XLA Ops:
  10.5 4.5 collective-permute-start
  39.8 2.4 fusion.109
  42.2 2.4 fusion.111
  44.6 2.4 convolution_subtract_fusion.15
  62.7 2.4 fusion.124
  65.1 2.4 fusion.126
  67.5 2.4 convolution_subtract_fusion.21
  73.1 2.4 convolution_add_fusion.69
  99.3 2.4 convolution_add_fusion.51
  148.8 2.4 fusion.143
  151.1 2.3 fusion.101
  153.5 2.4 convolution_add_fusion.39
  172.5 2.3 fusion.149
  174.9 2.3 fusion.116
  177.2 2.4 convolution_add_fusion.57
  183.4 2.3 convolution_add_fusion.38
  189.1 2.3 convolution_add_fusion.56
  194.2 3.0 fusion.28
  199.7 13.7 %dynamic_update_slice.16 = f32[2,2,320,384]{3,2,1,0:T(8,128)S(1)} dynamic-update-slice(f32[2,2,320,384]{3,2,1,0:T(8,128)S(1)} %broadcast.211.clone, f32[2,2,256,256]{3,2,1,0:T(8,128)} %pad_add_fusion.1, s32[]{:T(128)} %constant.146.clone.1, s32[]{:T(128)} %constant.146.clone.1, s32[]{:T(128)S(6)} %select_n.600, s32[]{:T(128)S(6)} %select_n.601) | dynamic-update-slice | bytes 2097156 | tf_op jit(solution)/shard_map/transpose(jvp())/dynamic_update_slice | solution.py:73
  213.4 2.7 add_add_fusion.1
  216.1 14.4 %add_any.440 = f32[2,2,320,384]{3,2,1,0:T(8,128)S(1)} dynamic-update-slice(f32[2,2,320,384]{3,2,1,0:T(8,128)S(1)} %dynamic_update_slice.16, f32[2,2,256,256]{3,2,1,0:T(8,128)} %add_add_fusion.1, s32[]{:T(128)} %constant.146.clone.1, s32[]{:T(128)} %constant.146.clone.1, s32[]{:T(128)S(6)} %select_n.609, s32[]{:T(128)S(6)} %select_n.610) | dynamic-update-slice | bytes 2097156 | tf_op jit(solution)/shard_map/transpose(jvp())/add_any | solution.py:73
  233.5 3.1 collective-permute-start.3
  248.5 2.4 collective-permute-start.5
  250.9 82.3 %all-reduce.48.cloned.1.call-done = (f32[2,256,256]{2,1,0:T(8,128)}, f32[1,256,256]{2,1,0:T(8,128)}) async-done(((f32[2,256,256]{2,1,0:T(8,128)}, f32[1,256,256]{2,1,0:T(8,128)}), (f32[2,256,256]{2,1,0:T(8,128)}, f32[1,256,256]{2,1,0:T(8,128)})) %all-reduce.48.cloned.1.call-update) | async-done | bytes 786448 | tf_op jit(solution)/shard_map/psum | solution.py:109
  348.5 2.4 fusion.79
  350.9 2.4 fusion.81
  353.3 2.4 convolution_subtract_fusion.3
  357.1 2.5 fusion.80
  371.6 2.4 fusion.94
  374.0 2.4 fusion.96
  376.4 2.4 convolution_subtract_fusion.9
  381.7 2.4 convolution_add_fusion.33
  425.8 2.3 fusion.137
  428.1 2.3 fusion.86
  430.5 2.3 convolution_add_fusion.21
  436.7 2.4 convolution_add_fusion.15
  453.0 2.6 multiply_reduce_fusion.2
  482.2 2.4 fusion.131
  484.6 2.3 fusion.71
  486.9 2.4 convolution_add_fusion.3
  503.8 3.0 fusion.16
  510.3 13.7 %dynamic_update_slice.19 = f32[2,2,320,384]{3,2,1,0:T(8,128)S(1)} dynamic-update-slice(f32[2,2,320,384]{3,2,1,0:T(8,128)S(1)} %broadcast.211, f32[2,2,256,256]{3,2,1,0:T(8,128)} %pad_add_fusion, s32[]{:T(128)} %constant.146.clone.1, s32[]{:T(128)} %constant.146.clone.1, s32[]{:T(128)S(6)} %select_n.600, s32[]{:T(128)S(6)} %select_n.601) | dynamic-update-slice | bytes 2097156 | tf_op jit(solution)/shard_map/transpose(jvp())/dynamic_update_slice | solution.py:73
  524.0 2.9 add_add_fusion
  526.9 13.9 %add_any.504 = f32[2,2,320,384]{3,2,1,0:T(8,128)S(1)} dynamic-update-slice(f32[2,2,320,384]{3,2,1,0:T(8,128)S(1)} %dynamic_update_slice.19, f32[2,2,256,256]{3,2,1,0:T(8,128)} %add_add_fusion, s32[]{:T(128)} %constant.146.clone.1, s32[]{:T(128)} %constant.146.clone.1, s32[]{:T(128)S(6)} %select_n.609, s32[]{:T(128)S(6)} %select_n.610) | dynamic-update-slice | bytes 2097156 | tf_op jit(solution)/shard_map/transpose(jvp())/add_any | solution.py:73
  541.8 4.2 collective-permute-start.6
  550.2 28.6 %all-reduce.40 = (f32[]{:T(128)}, f32[]{:T(128)}) all-reduce(f32[]{:T(128)S(6)} %add.1009, f32[]{:T(128)S(6)} %add.1008), channel_id=1, replica_groups=mesh['scan'=2,'row'=16] {'row'}, use_global_device_ids=true, to_apply=%region_11.12 | all-reduce | flops 2 | bytes 16 | tf_op jit(solution)/shard_map/psum | solution.py:109
  582.0 4.2 collective-permute-start.7
  588.5 49.5 %all-reduce.46.cloned.1.call-done = (f32[2,256,256]{2,1,0:T(8,128)}, f32[1,256,256]{2,1,0:T(8,128)}) async-done(((f32[2,256,256]{2,1,0:T(8,128)}, f32[1,256,256]{2,1,0:T(8,128)}), (f32[2,256,256]{2,1,0:T(8,128)}, f32[1,256,256]{2,1,0:T(8,128)})) %all-reduce.46.cloned.1.call-update) | async-done | bytes 786448 | tf_op jit(solution)/shard_map/psum | solution.py:109
  (289 shorter events, 297.1 us)
Async XLA Ops:
  7.2 18.8 %copy-start.2 = (f32[2,2,192,384]{3,2,1,0:T(8,128)S(1)}, f32[2,2,192,384]{3,2,1,0:T(8,128)}, u32[]{:S(2)}) copy-start(f32[2,2,192,384]{3,2,1,0:T(8,128)} %param.14) | copy-start | bytes 3538948
  7.2 7.8 %copy-start.20 = (s32[2]{0:T(128)S(1)}, s32[2]{0:T(128)}, u32[]{:S(2)}) copy-start(s32[2]{0:T(128)} %param.17) | copy-start | bytes 28
  7.2 8.4 %copy-start.21 = (s32[2]{0:T(128)S(1)}, s32[2]{0:T(128)}, u32[]{:S(2)}) copy-start(s32[2]{0:T(128)} %param.18) | copy-start | bytes 28
  7.2 9.0 %copy-start.22 = (s32[2]{0:T(128)S(1)}, s32[2]{0:T(128)}, u32[]{:S(2)}) copy-start(s32[2]{0:T(128)} %param.19) | copy-start | bytes 28
  7.2 326.0 %all-reduce.48.cloned.1.call-start = ((), (), s32[]{:S(2)}) async-start(), calls=%async_computation.1 | async-start | bytes 1572864 | tf_op jit(solution)/shard_map/psum | solution.py:109
  8.5 17.6 %collective-permute-start.1 = (f32[2,2,64,384]{3,2,1,0:T(8,128)S(1)}, f32[2,2,64,384]{3,2,1,0:T(8,128)S(1)}, u32[]{:S(2)}, u32[]{:S(2)}) collective-permute-start(f32[2,2,64,384]{3,2,1,0:T(8,128)S(1)} %get-tuple-element.75), channel_id=1, source_target_pairs={{1,0},{2,1},{3,2},{4,3},{5,4},{6,5},{7,6},{8,7},{9,8},{10,9},{11,1... | collective-permute-start | bytes 1179656 | tf_op jit(solution)/shard_map/ppermute | solution.py:26
  10.5 15.5 %collective-permute-start = (f32[2,2,64,384]{3,2,1,0:T(8,128)S(1)}, f32[2,2,64,384]{3,2,1,0:T(8,128)S(1)}, u32[]{:S(2)}, u32[]{:S(2)}) collective-permute-start(f32[2,2,64,384]{3,2,1,0:T(8,128)S(1)} %get-tuple-element.76), channel_id=1, source_target_pairs={{0,1},{1,2},{2,3},{3,4},{4,5},{5,6},{6,7},{7,8},{8,9},{9,10},{10,1... | collective-permute-start | bytes 1179656 | tf_op jit(solution)/shard_map/ppermute | solution.py:25
  26.2 1.0 copy-start.8
  87.8 2.8 copy-start.23
  89.2 36.4 %copy-start.29 = (f32[256,256]{1,0:T(8,128)}, f32[256,256]{1,0:T(8,128)S(1)}, u32[]{:S(2)}) copy-start(f32[256,256]{1,0:T(8,128)S(1)} %convolution_subtract_fusion.18) | copy-start | bytes 786436
  90.5 35.1 %copy-start.25 = (f32[256,256]{1,0:T(8,128)}, f32[256,256]{1,0:T(8,128)S(1)}, u32[]{:S(2)}) copy-start(f32[256,256]{1,0:T(8,128)S(1)} %convolution_add_fusion.66) | copy-start | bytes 786436
  115.5 15.1 %copy-start.31 = (f32[256,256]{1,0:T(8,128)}, f32[256,256]{1,0:T(8,128)S(1)}, u32[]{:S(2)}) copy-start(f32[256,256]{1,0:T(8,128)S(1)} %convolution_subtract_fusion.12) | copy-start | bytes 786436
  116.9 13.7 %copy-start.27 = (f32[256,256]{1,0:T(8,128)}, f32[256,256]{1,0:T(8,128)S(1)}, u32[]{:S(2)}) copy-start(f32[256,256]{1,0:T(8,128)S(1)} %convolution_add_fusion.48) | copy-start | bytes 786436
  187.6 6.6 %copy-start.10 = (f32[256,256]{1,0:T(8,128)}, f32[256,256]{1,0:T(8,128)S(1)}, u32[]{:S(2)}) copy-start(f32[256,256]{1,0:T(8,128)S(1)} %convolution_add_fusion.36) | copy-start | bytes 786436
  189.1 5.1 copy-start.12
  230.5 3.0 copy-start.11
  230.5 3.0 copy-start.13
  231.5 8.7 %collective-permute-start.2 = (f32[2,2,64,384]{3,2,1,0:T(8,128)}, f32[2,2,64,384]{3,2,1,0:T(8,128)}, u32[]{:S(2)}, u32[]{:S(2)}) collective-permute-start(f32[2,2,64,384]{3,2,1,0:T(8,128)} %get-tuple-element.68), channel_id=1, source_target_pairs={{0,1},{1,2},{2,3},{3,4},{4,5},{5,6},{6,7},{7,8},{8,9},{9,10},{10,1... | collective-permute-start | bytes 1179656 | tf_op jit(solution)/shard_map/ppermute | solution.py:25
  233.5 9.5 %collective-permute-start.3 = (f32[2,2,64,384]{3,2,1,0:T(8,128)}, f32[2,2,64,384]{3,2,1,0:T(8,128)}, u32[]{:S(2)}, u32[]{:S(2)}) collective-permute-start(f32[2,2,64,384]{3,2,1,0:T(8,128)} %get-tuple-element.67), channel_id=1, source_target_pairs={{1,0},{2,1},{3,2},{4,3},{5,4},{6,5},{7,6},{8,7},{9,8},{10,9},{11,1... | collective-permute-start | bytes 1179656 | tf_op jit(solution)/shard_map/ppermute | solution.py:26
  237.4 1.8 copy-start.14
  237.4 1.8 copy-start.15
  240.1 4.9 copy-start.3
  240.1 397.9 %all-reduce.46.cloned.1.call-start = ((), (), s32[]{:S(2)}) async-start(), calls=%async_computation | async-start | bytes 1572864 | tf_op jit(solution)/shard_map/psum | solution.py:109
  246.4 87.8 %copy-start.9 = (f32[2,256,256]{2,1,0:T(8,128)S(1)}, f32[2,256,256]{2,1,0:T(8,128)}, u32[]{:S(2)}) copy-start(f32[2,256,256]{2,1,0:T(8,128)} %param.15) | copy-start | bytes 1572868
  246.4 88.9 %collective-permute-start.4 = (f32[2,2,64,384]{3,2,1,0:T(8,128)S(1)}, f32[2,2,64,384]{3,2,1,0:T(8,128)S(1)}, u32[]{:S(2)}, u32[]{:S(2)}) collective-permute-start(f32[2,2,64,384]{3,2,1,0:T(8,128)S(1)} %get-tuple-element.73), channel_id=1, source_target_pairs={{0,1},{1,2},{2,3},{3,4},{4,5},{5,6},{6,7},{7,8},{8,9},{9,10},{10,1... | collective-permute-start | bytes 1179656 | tf_op jit(solution)/shard_map/ppermute | solution.py:25
  248.5 86.9 %collective-permute-start.5 = (f32[2,2,64,384]{3,2,1,0:T(8,128)S(1)}, f32[2,2,64,384]{3,2,1,0:T(8,128)S(1)}, u32[]{:S(2)}, u32[]{:S(2)}) collective-permute-start(f32[2,2,64,384]{3,2,1,0:T(8,128)S(1)} %get-tuple-element.74), channel_id=1, source_target_pairs={{1,0},{2,1},{3,2},{4,3},{5,4},{6,5},{7,6},{8,7},{9,8},{10,9},{11,1... | collective-permute-start | bytes 1179656 | tf_op jit(solution)/shard_map/ppermute | solution.py:26
  335.3 168.4 %copy-start.4 = (f32[2,256,256]{2,1,0:T(8,128)}, f32[2,256,256]{2,1,0:T(8,128)S(1)}, u32[]{:S(2)}) copy-start(f32[2,256,256]{2,1,0:T(8,128)S(1)} %divide_subtract_fusion.1) | copy-start | bytes 1572868
  336.1 166.7 %copy-start = (f32[1,2,256,256]{3,2,1,0:T(8,128)}, f32[1,2,256,256]{3,2,1,0:T(8,128)S(1)}, u32[]{:S(2)}) copy-start(f32[1,2,256,256]{3,2,1,0:T(8,128)S(1)} %get-tuple-element.64) | copy-start | bytes 1572868
  336.2 167.6 %copy-start.5 = (f32[1,2,256,256]{3,2,1,0:T(8,128)}, f32[1,2,256,256]{3,2,1,0:T(8,128)S(1)}, u32[]{:S(2)}) copy-start(f32[1,2,256,256]{3,2,1,0:T(8,128)S(1)} %get-tuple-element.65) | copy-start | bytes 1572868
  396.4 2.8 copy-start.24
  449.5 3.5 copy-start.26
  449.5 3.5 copy-start.28
  449.5 3.5 copy-start.30
  449.5 3.5 copy-start.32
  540.8 5.2 copy-start.16
  540.8 5.2 copy-start.17
  540.9 5.2 copy-start.18
  541.8 5.1 copy-start.1
  541.8 5.1 copy-start.6
  541.8 44.9 %collective-permute-start.6 = (f32[2,2,64,384]{3,2,1,0:T(8,128)}, f32[2,2,64,384]{3,2,1,0:T(8,128)}, u32[]{:S(2)}, u32[]{:S(2)}) collective-permute-start(f32[2,2,64,384]{3,2,1,0:T(8,128)} %get-tuple-element.62), channel_id=1, source_target_pairs={{0,1},{1,2},{2,3},{3,4},{4,5},{5,6},{6,7},{7,8},{8,9},{9,10},{10,1... | collective-permute-start | bytes 1179656 | tf_op jit(solution)/shard_map/ppermute | solution.py:25
  578.8 3.1 copy-start.19
  582.0 59.2 %collective-permute-start.7 = (f32[2,2,64,384]{3,2,1,0:T(8,128)S(1)}, f32[2,2,64,384]{3,2,1,0:T(8,128)}, u32[]{:S(2)}, u32[]{:S(2)}) collective-permute-start(f32[2,2,64,384]{3,2,1,0:T(8,128)S(1)} %copy-done.19), channel_id=1, source_target_pairs={{1,0},{2,1},{3,2},{4,3},{5,4},{6,5},{7,6},{8,7},{9,8},{10,9},{11,1... | collective-permute-start | bytes 1179656 | tf_op jit(solution)/shard_map/ppermute | solution.py:26
  638.0 3.2 copy-start.7
Sparse Core Ops, SparseCore 0:
  240.2 92.9 all-reduce.47
  547.8 90.1 all-reduce.45
where the time goes:
time: 659 us; the launch traced here: 650 us
  matrix products  336 us (51%)
  waiting for transfers between devices  133 us (20%)
  local copies, waits for them, and re-layouts  63.8 us (10%)
  other arithmetic  33.7 us (5%)
  between operations  30.8 us (5%)
  blocking collectives  28.6 us (4%)
  starting transfers between devices  24.4 us (4%)
    dot_general x192, matrix products, matmul(): jnp.dot(left, right, precision=lax.Precision.HIGHEST, preferred_element_t...  336 us
    psum x2, waiting for transfers between devices, renew_probe(): lax.psum((grad_probe, weight, total), 'row')  132 us
    psum x1, blocking collectives, renew_probe(): lax.psum((grad_probe, weight, total), 'row')  28.6 us
    add_any x2, local copies, waits for them, and re-layouts, objective(): lax.dynamic_slice(extended, (anchor, anchor, row_offset[index], col_offse...  28.3 us
    dynamic_update_slice x2, local copies, waits for them, and re-layouts, objective(): lax.dynamic_slice(extended, (anchor, anchor, row_offset[index], col_offse...  27.3 us
  transfers between devices with their start and end apart: 10, of which 3 were waited for; matrix products, arithmetic and copies ran while one was open for 3% of the time, Pallas kernels for 0%

commit v1 on v0

v1 whole, which is shorter than its diff:
```python
import functools

import jax
import jax.numpy as jnp
import ml_dtypes
import numpy as np
from jax import lax
from jax.experimental import pallas as pl
from jax.experimental.pallas import tpu as pltpu
from jax.sharding import PartitionSpec as P

MARGIN = 64
ITERS = 2
SMOOTHING = 0.01
OBJECT_RATE = 0.25
PROBE_RATE = 0.5
PROPAGATION = 4.0
DAMPING = 1.0
TINY = 1e-06


def split_table(table):
    left = np.block([[table.real, -table.imag], [table.imag, table.real]])
    high = left.astype(ml_dtypes.bfloat16)
    low = (left - high.astype(np.float64)).astype(ml_dtypes.bfloat16)
    on_left = np.concatenate([high, low, high], axis=1)
    on_right = np.concatenate([high.T, high.T, low.T], axis=0)
    return np.ascontiguousarray(on_left), np.ascontiguousarray(on_right)


@functools.lru_cache(maxsize=None)
def tables(length):
    counter = np.arange(length)
    dft = np.exp(-2j * np.pi / length * ((counter[:, None] * counter[None, :]) % length))
    dft = dft / np.sqrt(length)
    signed = np.where(counter < length // 2, counter, counter - length) / length
    phase = np.exp(-1j * np.pi * PROPAGATION * signed**2)
    spread = (np.conj(dft) * phase[None, :]) @ dft
    return split_table(dft) + split_table(spread)


def halves(value):
    high = value.astype(jnp.bfloat16)
    low = (value - high.astype(jnp.float32)).astype(jnp.bfloat16)
    return high, low


def both_sides(re, im, on_left, on_right):
    length = re.shape[0]
    high, low = halves(jnp.concatenate([re, im], axis=1))
    rows = jnp.dot(
        jnp.concatenate([high, low, high], axis=1),
        on_right[...],
        preferred_element_type=jnp.float32,
    )
    stacked = jnp.concatenate([rows[:, :length], rows[:, length:]], axis=0)
    high, low = halves(stacked)
    done = jnp.dot(
        on_left[...],
        jnp.concatenate([high, high, low], axis=0),
        preferred_element_type=jnp.float32,
    )
    return done[:length], done[length:]


def times(a_re, a_im, b_re, b_im):
    return a_re * b_re - a_im * b_im, a_re * b_im + a_im * b_re


def local_kernel(
    rows_ref, cols_ref, first_ref, field, probe, intensity, dft_l, dft_r, spread_l, spread_r,
    grad, sums, window,
):
    length = probe.shape[1]
    width = field.shape[3]
    grad[...] = jnp.zeros_like(grad)
    sums[...] = jnp.zeros_like(sums)

    @pl.loop(0, intensity.shape[0])
    def _(index):
        row = rows_ref[index]
        col = cols_ref[index]
        base = pl.multiple_of(jnp.minimum(row // 8 * 8, field.shape[2] - length - 8), 8)
        extra = row - base
        up = lax.rem(length + 8 - extra, length + 8)
        taken = pl.ds(base, length + 8)
        chosen = first_ref[index] == 0
        back = lax.rem(width - col, width)
        for which in range(2):
            for part in range(2):
                wide = pltpu.roll(field[which, part, taken, :], back, 1)[:, :length]
                window[which, part] = pltpu.roll(wide, up, 0)[:length]
        front_at = jnp.where(chosen, 0, 1)
        behind_at = 1 - front_at
        front_re, front_im = window[front_at, 0], window[front_at, 1]
        wave_re, wave_im = times(probe[0], probe[1], front_re, front_im)
        sums[2 * length : 3 * length] += front_re * front_re + front_im * front_im
        near_re, near_im = both_sides(wave_re, wave_im, spread_l, spread_r)
        exit_re, exit_im = times(near_re, near_im, window[behind_at, 0], window[behind_at, 1])
        far_re, far_im = both_sides(exit_re, exit_im, dft_l, dft_r)
        modulus = jnp.sqrt(far_re * far_re + far_im * far_im + SMOOTHING)
        misfit = modulus - jnp.sqrt(intensity[index] + SMOOTHING)
        squares = (misfit * misfit).reshape(length // 8, 8, length)
        sums[3 * length : 3 * length + 8] += jnp.sum(squares, axis=0)
        slope = 2.0 * misfit / modulus
        exit_re, exit_im = both_sides(slope * far_re, -slope * far_im, dft_l, dft_r)
        behind_re, behind_im = times(near_re, near_im, exit_re, exit_im)
        near_re, near_im = times(window[behind_at, 0], window[behind_at, 1], exit_re, exit_im)
        wave_re, wave_im = both_sides(near_re, near_im, spread_l, spread_r)
        probe_re, probe_im = times(window[front_at, 0], window[front_at, 1], wave_re, wave_im)
        sums[:length] += probe_re
        sums[length : 2 * length] -= probe_im
        front_re, front_im = times(probe[0], probe[1], wave_re, wave_im)
        below = jnp.zeros((8, length), jnp.float32)
        beside = jnp.zeros((length + 8, width - length), jnp.float32)
        for which, part, value in (
            (front_at, 0, front_re),
            (front_at, 1, -front_im),
            (behind_at, 0, behind_re),
            (behind_at, 1, -behind_im),
        ):
            value = pltpu.roll(jnp.concatenate([value, below], axis=0), extra, 0)
            wide = pltpu.roll(jnp.concatenate([value, beside], axis=1), col, 1)
            grad[which, part, taken, :] += wide


def local_terms(field, probe, intensity, rows, cols, first):
    length = probe.shape[1]
    vmem = pl.BlockSpec(memory_space=pltpu.VMEM)
    smem = pl.BlockSpec(memory_space=pltpu.SMEM)
    return pl.pallas_call(
        local_kernel,
        out_shape=(
            jax.ShapeDtypeStruct(field.shape, jnp.float32),
            jax.ShapeDtypeStruct((3 * length + 8, length), jnp.float32),
        ),
        in_specs=[smem] * 3 + [vmem] * 7,
        out_specs=(vmem, vmem),
        scratch_shapes=[pltpu.VMEM((2, 2, length, length), jnp.float32)],
        compiler_params=pltpu.CompilerParams(vmem_limit_bytes=48 * 1024 * 1024),
    )(rows, cols, first, field, probe, intensity, *(jnp.asarray(t) for t in tables(length)))


def from_sides(to_before, to_after):
    devices = lax.axis_size("row")
    up = [(i, i + 1) for i in range(devices - 1)]
    down = [(i + 1, i) for i in range(devices - 1)]
    return lax.ppermute(to_after, "row", up), lax.ppermute(to_before, "row", down)


def shards(object_field, probe, intensity, row_offset, col_offset, slice_first):
    length = probe.shape[1]
    tile = object_field.shape[2]
    count = intensity.shape[0] * lax.axis_size("row") * length * length
    before, after = from_sides(object_field[:, :, :MARGIN], object_field[:, :, tile - MARGIN :])
    field = jnp.concatenate([before, object_field, after], axis=2)
    here = lax.axis_index("row")
    inside = jnp.arange(tile + 2 * MARGIN)[:, None]
    inside = ((inside >= MARGIN) | (here > 0)) & (
        (inside < tile + MARGIN) | (here < lax.axis_size("row") - 1)
    )
    losses = []
    for step in range(ITERS):
        grad, sums = local_terms(field, probe, intensity, row_offset, col_offset, slice_first)
        rate = OBJECT_RATE / (jnp.mean(probe[0] * probe[0] + probe[1] * probe[1]) + TINY)
        sums = lax.psum(sums, "row")
        if step < ITERS - 1:
            before, after = from_sides(grad[:, :, : 2 * MARGIN], grad[:, :, tile:])
            middle = jnp.zeros_like(grad[:, :, : tile - 2 * MARGIN])
            grad = grad + jnp.concatenate([before, middle, after], axis=2)
            field = jnp.where(inside, field - rate * grad, 0.0)
        else:
            before, after = from_sides(grad[:, :, :MARGIN], grad[:, :, tile + MARGIN :])
            middle = jnp.zeros_like(grad[:, :, : tile - 2 * MARGIN])
            grad = grad[:, :, MARGIN : tile + MARGIN] + jnp.concatenate(
                [before, middle, after], axis=2
            )
            field = field[:, :, MARGIN : tile + MARGIN] - rate * grad
        summed = sums[: 2 * length].reshape(2, length, length)
        weight = sums[2 * length : 3 * length]
        probe = probe - PROBE_RATE * summed / (weight + DAMPING)
        losses.append(jnp.sum(sums[3 * length :]) / count)
    return field, probe, jnp.stack(losses)


def solution(mesh):
    placed = (
        P("scan", None, "row", None),
        P("scan", None, None),
        P(("scan", "row"), None, None),
        P(("scan", "row")),
        P(("scan", "row")),
        P(("scan", "row")),
    )
    return jax.shard_map(
        shards,
        mesh=mesh,
        in_specs=placed,
        out_specs=(P("scan", None, "row", None), P("scan", None, None), P("scan")),
        check_vma=False,
    )
```

time: 659 us -> 280 us (0.42); the launches traced: 650 us -> 279 us
  matrix products: 336 us -> 0 us
  local copies, waits for them, and re-layouts: 63.8 us -> 8.46 us
  waiting for transfers between devices: 133 us -> 183 us
  Pallas kernels: 0 us -> 38.7 us
  blocking collectives: 28.6 us -> 0 us
  other arithmetic: 33.7 us -> 16.1 us
  between operations: 30.8 us -> 17 us
  starting transfers between devices: 24.4 us -> 16.5 us
    dot_general x192 -> x0, matrix products: 336 us -> none  [matmul(): jnp.dot(left, right, precision=lax.Precision.HIGHEST, preferred_element_t...]
    psum x2, waiting for transfers between devices: 132 us -> 172 us  [shards(): sums = lax.psum(sums, 'row')]
    pallas_call x0 -> x2, Pallas kernels: none -> 38.7 us  [local_terms(): pl.pallas_call(local_kernel, out_shape=(jax.ShapeDtypeStruct(field.shape,...]
    psum x1 -> x0, blocking collectives: 28.6 us -> none  [renew_probe(): lax.psum((grad_probe, weight, total), 'row')]
    add_any x2 -> x0, local copies, waits for them, and re-layouts: 28.3 us -> none  [objective(): lax.dynamic_slice(extended, (anchor, anchor, row_offset[index], col_offse...]
    dynamic_update_slice x2 -> x0, local copies, waits for them, and re-layouts: 27.3 us -> none  [objective(): lax.dynamic_slice(extended, (anchor, anchor, row_offset[index], col_offse...]
    ppermute x8 -> x6, waiting for transfers between devices: 1.05 us -> 10.9 us  [the longest x3 8.49 us: from_sides(): lax.ppermute(to_before, 'row', down)]
    ppermute x8 -> x6, starting transfers between devices: 24.4 us -> 16.4 us  [the longest x3 8.61 us: from_sides(): lax.ppermute(to_after, 'row', up)]
  transfers between devices with their start and end apart: 10 -> 8, of which waited for: 3 -> 5; matrix products, arithmetic and copies ran while one was open for 3% -> 4% of each run, Pallas kernels for 0% -> 0%
where the time goes in v1:
time: 280 us; the launch traced here: 279 us
  waiting for transfers between devices  183 us (65%)
  Pallas kernels  38.7 us (14%)
  between operations  17 us (6%)
  starting transfers between devices  16.5 us (6%)
  other arithmetic  16.1 us (6%)
  local copies, waits for them, and re-layouts  8.46 us (3%)
    psum x2, waiting for transfers between devices, shards(): sums = lax.psum(sums, 'row')  172 us
    pallas_call x2, Pallas kernels, local_terms(): pl.pallas_call(local_kernel, out_shape=(jax.ShapeDtypeStruct(field.shape,...  38.7 us
    ppermute x3, starting transfers between devices, from_sides(): lax.ppermute(to_after, 'row', up)  8.61 us
    ppermute x3, waiting for transfers between devices, from_sides(): lax.ppermute(to_before, 'row', down)  8.49 us
    ppermute x3, starting transfers between devices, from_sides(): lax.ppermute(to_before, 'row', down)  7.8 us
  transfers between devices with their start and end apart: 8, of which 5 were waited for; matrix products, arithmetic and copies ran while one was open for 4% of the time, Pallas kernels for 0%

profile of v1, /device:TPU:1, one launch (start us, length us, event | category | flops | bytes accessed | tf_op | source)
XLA Modules:
  0.0 279.3 jit_solution(18262845239663259817)
XLA Ops:
  7.2 0.0 all-reduce.3.cloned.1.call-start
  7.2 0.0 copy-start.12
  7.2 0.0 copy-start.4
  7.2 1.3 fusion.11
  8.5 4.5 %collective-permute-start = (f32[2,2,64,384]{3,2,1,0:T(8,128)S(1)}, f32[2,2,64,384]{3,2,1,0:T(8,128)S(1)}, u32[]{:S(2)}, u32[]{:S(2)}) collective-permute-start(f32[2,2,64,384]{3,2,1,0:T(8,128)S(1)} %get-tuple-element.16), channel_id=1, source_target_pairs={{0,1},{1,2},{2,3},{3,4},{4,5},{5,6},{6,7},{7,8},{8,9},{9,10},{10,1... | collective-permute-start | bytes 1179656 | tf_op jit(solution)/shard_map/ppermute | solution.py:148
  13.1 0.0 copy-start
  13.1 0.0 copy-start.1
  13.1 0.0 copy-start.3
  13.1 0.0 copy-start.6
  13.1 0.0 copy-start.7
  13.1 0.0 copy-start.8
  13.1 2.2 collective-permute-start.1
  15.3 2.4 collective-permute-done
  17.8 0.1 constant_dynamic-update-slice_fusion.1
  17.9 4.6 %collective-permute-done.1 = f32[2,2,64,384]{3,2,1,0:T(8,128)S(1)} collective-permute-done((f32[2,2,64,384]{3,2,1,0:T(8,128)S(1)}, f32[2,2,64,384]{3,2,1,0:T(8,128)S(1)}, u32[]{:S(2)}, u32[]{:S(2)}) %collective-permute-start.1) | collective-permute-done | bytes 393248 | tf_op jit(solution)/shard_map/ppermute | solution.py:148
  22.5 1.2 copy-done.10
  23.8 19.3 %shard_map.121 = (f32[2,2,320,384]{3,2,1,0:T(8,128)}, f32[776,256]{1,0:T(8,128)S(1)}) custom-call(s32[2]{0:T(128)S(1)} %copy-done.6, s32[2]{0:T(128)S(1)} %copy-done.7, s32[2]{0:T(128)S(1)} %copy-done.8, f32[2,2,320,384]{3,2,1,0:T(8,128)} %copy-done.10, f32[2,256,256]{2,1,0:T(8,128)S(1)} %copy-done.3, f32[2,256,256]{2,1,0:T(8,128)S(1)} %copy-done.4, ...), custom_call_target="tpu_custom_call" | custom-call | tf_op jit(solution)/shard_map/pallas_call | solution.py:131
  43.2 0.9 copy-done.5
  44.1 0.0 all-reduce.3.cloned.1.call-update
  44.1 0.0 all-reduce.5.cloned.1.call-start
  44.1 0.7 add_reduce_fusion
  44.8 2.6 fusion.10
  47.4 1.9 collective-permute-start.2
  49.4 3.5 %collective-permute-start.3 = (f32[2,2,128,384]{3,2,1,0:T(8,128)}, f32[2,2,128,384]{3,2,1,0:T(8,128)}, u32[]{:S(2)}, u32[]{:S(2)}) collective-permute-start(f32[2,2,128,384]{3,2,1,0:T(8,128)} %get-tuple-element.14), channel_id=1, source_target_pairs={{1,0},{2,1},{3,2},{4,3},{5,4},{6,5},{7,6},{8,7},{9,8},{10,9},{11,1... | collective-permute-start | bytes 2359304 | tf_op jit(solution)/shard_map/ppermute | solution.py:148
  53.5 85.9 %all-reduce.3.cloned.1.call-done = f32[776,256]{1,0:T(8,128)} async-done(((f32[776,256]{1,0:T(8,128)}), f32[776,256]{1,0:T(8,128)}) %all-reduce.3.cloned.1.call-update) | async-done | bytes 794640 | tf_op jit(solution)/shard_map/psum | solution.py:166
  139.4 1.1 slice_add_fusion.1
  140.6 1.1 slice_multiply_fusion.1
  141.6 0.1 divide_subtract_fusion.1.probe
  141.7 0.0 collective-permute-done.2
  141.7 0.0 collective-permute-done.3
  141.8 0.0 copy-start.2
  141.8 3.8 %fusion.2.field = f32[2,2,320,384]{3,2,1,0:T(8,128)} fusion(f32[2,2,320,384]{3,2,1,0:T(8,128)S(1)} %copy-done.11, f32[2,2,320,384]{3,2,1,0:T(8,128)} %get-tuple-element.7, f32[2,2,128,384]{3,2,1,0:T(8,128)} %collective-permute-done.3, f32[2,2,64,384]{3,2,1,0:T(8,128)S(1)} %broadcast.29, f32[2,2,128,384]{3,2,1,0:T(8,128)} %collective-permute-done.2, ...), kind=kLoop, calls=%fused_computation.3 | loop fusion | flops 2949120 | bytes 7864644 | tf_op jit(solution)/shard_map/jit(_where)/select_n | solution.py:171
  145.6 19.3 %shard_map.122 = (f32[2,2,320,384]{3,2,1,0:T(8,128)}, f32[776,256]{1,0:T(8,128)}) custom-call(s32[2]{0:T(128)S(1)} %copy-done.6, s32[2]{0:T(128)S(1)} %copy-done.7, s32[2]{0:T(128)S(1)} %copy-done.8, f32[2,2,320,384]{3,2,1,0:T(8,128)} %fusion.2.field, f32[2,256,256]{2,1,0:T(8,128)S(1)} %divide_subtract_fusion.1.probe, f32[2,256,256]{2,1,0:T(8,128)S(1)} %copy-done.4, ...), custom_call_target="tpu_custom_call" | custom-call | tf_op jit(solution)/shard_map/pallas_call | solution.py:131
  164.9 2.2 fusion.9
  167.1 2.2 collective-permute-start.4
  169.3 2.2 collective-permute-start.5
  171.5 0.7 fusion.5
  172.8 0.0 all-reduce.5.cloned.1.call-update
  172.8 1.3 slice_reduce_fusion.1
  174.8 0.0 collective-permute-done.4
  174.8 3.9 %collective-permute-done.5 = f32[2,2,64,384]{3,2,1,0:T(8,128)} collective-permute-done((f32[2,2,64,384]{3,2,1,0:T(8,128)}, f32[2,2,64,384]{3,2,1,0:T(8,128)}, u32[]{:S(2)}, u32[]{:S(2)}) %collective-permute-start.5) | collective-permute-done | bytes 393248 | tf_op jit(solution)/shard_map/ppermute | solution.py:148
  178.7 2.6 slice_subtract_fusion
  181.3 85.6 %all-reduce.5.cloned.1.call-done = f32[776,256]{1,0:T(8,128)} async-done(((f32[776,256]{1,0:T(8,128)}), f32[776,256]{1,0:T(8,128)}) %all-reduce.5.cloned.1.call-update) | async-done | bytes 794640 | tf_op jit(solution)/shard_map/psum | solution.py:166
  267.0 1.3 slice_reduce_fusion
  268.9 0.6 pad_maximum_fusion
  269.5 1.0 slice_add_fusion
  270.5 1.1 slice_multiply_fusion
  271.6 0.9 divide_subtract_fusion
  (19 shorter events, 0.1 us)
Async XLA Ops:
  7.2 132.3 %all-reduce.3.cloned.1.call-start = ((), (), s32[]{:S(2)}) async-start(), calls=%async_computation | async-start | bytes 1589248 | tf_op jit(solution)/shard_map/psum | solution.py:166
  7.2 10.6 %copy-start.12 = (f32[2,2,192,384]{3,2,1,0:T(8,128)S(1)}, f32[2,2,192,384]{3,2,1,0:T(8,128)}, u32[]{:S(2)}) copy-start(f32[2,2,192,384]{3,2,1,0:T(8,128)} %param.10) | copy-start | bytes 3538948
  7.2 16.6 %copy-start.4 = (f32[2,256,256]{2,1,0:T(8,128)S(1)}, f32[2,256,256]{2,1,0:T(8,128)}, u32[]{:S(2)}) copy-start(f32[2,256,256]{2,1,0:T(8,128)} %intensity.3) | copy-start | bytes 1572868
  8.5 9.2 %collective-permute-start = (f32[2,2,64,384]{3,2,1,0:T(8,128)S(1)}, f32[2,2,64,384]{3,2,1,0:T(8,128)S(1)}, u32[]{:S(2)}, u32[]{:S(2)}) collective-permute-start(f32[2,2,64,384]{3,2,1,0:T(8,128)S(1)} %get-tuple-element.16), channel_id=1, source_target_pairs={{0,1},{1,2},{2,3},{3,4},{4,5},{5,6},{6,7},{7,8},{8,9},{9,10},{10,1... | collective-permute-start | bytes 1179656 | tf_op jit(solution)/shard_map/ppermute | solution.py:148
  13.1 10.7 %copy-start = (bf16[1536,512]{1,0:T(8,128)(2,1)S(1)}, bf16[1536,512]{1,0:T(8,128)(2,1)}, u32[]{:S(2)}) copy-start(bf16[1536,512]{1,0:T(8,128)(2,1)} %constant.40.clone.dft_r) | copy-start | bytes 4718596
  13.1 10.7 %copy-start.1 = (bf16[512,1536]{1,0:T(8,128)(2,1)S(1)}, bf16[512,1536]{1,0:T(8,128)(2,1)}, u32[]{:S(2)}) copy-start(bf16[512,1536]{1,0:T(8,128)(2,1)} %constant.39.clone.dft_l) | copy-start | bytes 4718596
  13.1 10.7 %copy-start.3 = (f32[2,256,256]{2,1,0:T(8,128)S(1)}, f32[2,256,256]{2,1,0:T(8,128)}, u32[]{:S(2)}) copy-start(f32[2,256,256]{2,1,0:T(8,128)} %probe.1) | copy-start | bytes 1572868
  13.1 10.7 %copy-start.6 = (s32[2]{0:T(128)S(1)}, s32[2]{0:T(128)}, u32[]{:S(2)}) copy-start(s32[2]{0:T(128)} %rows_ref.3) | copy-start | bytes 28
  13.1 10.7 %copy-start.7 = (s32[2]{0:T(128)S(1)}, s32[2]{0:T(128)}, u32[]{:S(2)}) copy-start(s32[2]{0:T(128)} %cols_ref.3) | copy-start | bytes 28
  13.1 10.7 %copy-start.8 = (s32[2]{0:T(128)S(1)}, s32[2]{0:T(128)}, u32[]{:S(2)}) copy-start(s32[2]{0:T(128)} %first_ref.3) | copy-start | bytes 28
  13.1 9.4 %collective-permute-start.1 = (f32[2,2,64,384]{3,2,1,0:T(8,128)S(1)}, f32[2,2,64,384]{3,2,1,0:T(8,128)S(1)}, u32[]{:S(2)}, u32[]{:S(2)}) collective-permute-start(f32[2,2,64,384]{3,2,1,0:T(8,128)S(1)} %get-tuple-element.15), channel_id=1, source_target_pairs={{1,0},{2,1},{3,2},{4,3},{5,4},{6,5},{7,6},{8,7},{9,8},{10,9},{11,1... | collective-permute-start | bytes 1179656 | tf_op jit(solution)/shard_map/ppermute | solution.py:148
  22.5 1.3 copy-start.10
  43.2 0.9 copy-start.5
  44.1 222.9 %all-reduce.5.cloned.1.call-start = ((), (), s32[]{:S(2)}) async-start(), calls=%async_computation.1 | async-start | bytes 1589248 | tf_op jit(solution)/shard_map/psum | solution.py:166
  47.4 94.3 %collective-permute-start.2 = (f32[2,2,128,384]{3,2,1,0:T(8,128)}, f32[2,2,128,384]{3,2,1,0:T(8,128)}, u32[]{:S(2)}, u32[]{:S(2)}) collective-permute-start(f32[2,2,128,384]{3,2,1,0:T(8,128)} %get-tuple-element.13), channel_id=1, source_target_pairs={{0,1},{1,2},{2,3},{3,4},{4,5},{5,6},{6,7},{7,8},{8,9},{9,10},{10,1... | collective-permute-start | bytes 2359304 | tf_op jit(solution)/shard_map/ppermute | solution.py:148
  49.4 92.4 %collective-permute-start.3 = (f32[2,2,128,384]{3,2,1,0:T(8,128)}, f32[2,2,128,384]{3,2,1,0:T(8,128)}, u32[]{:S(2)}, u32[]{:S(2)}) collective-permute-start(f32[2,2,128,384]{3,2,1,0:T(8,128)} %get-tuple-element.14), channel_id=1, source_target_pairs={{1,0},{2,1},{3,2},{4,3},{5,4},{6,5},{7,6},{8,7},{9,8},{10,9},{11,1... | collective-permute-start | bytes 2359304 | tf_op jit(solution)/shard_map/ppermute | solution.py:148
  139.4 2.3 copy-start.11
  141.8 3.8 %copy-start.2 = (bf16[512,1536]{1,0:T(8,128)(2,1)S(1)}, bf16[512,1536]{1,0:T(8,128)(2,1)}, u32[]{:S(2)}) copy-start(bf16[512,1536]{1,0:T(8,128)(2,1)} %constant.39.clone.dft_l) | copy-start | bytes 4718596
  164.9 13.8 %copy-start.9 = (f32[2,2,320,384]{3,2,1,0:T(8,128)S(1)}, f32[2,2,320,384]{3,2,1,0:T(8,128)}, u32[]{:S(2)}) copy-start(f32[2,2,320,384]{3,2,1,0:T(8,128)} %fusion.2.field) | copy-start | bytes 5898244
  167.1 7.7 %collective-permute-start.4 = (f32[2,2,64,384]{3,2,1,0:T(8,128)}, f32[2,2,64,384]{3,2,1,0:T(8,128)S(1)}, u32[]{:S(2)}, u32[]{:S(2)}) collective-permute-start(f32[2,2,64,384]{3,2,1,0:T(8,128)} %get-tuple-element.11), channel_id=1, source_target_pairs={{0,1},{1,2},{2,3},{3,4},{4,5},{5,6},{6,7},{7,8},{8,9},{9,10},{10,1... | collective-permute-start | bytes 1179656 | tf_op jit(solution)/shard_map/ppermute | solution.py:148
  169.3 9.4 %collective-permute-start.5 = (f32[2,2,64,384]{3,2,1,0:T(8,128)}, f32[2,2,64,384]{3,2,1,0:T(8,128)}, u32[]{:S(2)}, u32[]{:S(2)}) collective-permute-start(f32[2,2,64,384]{3,2,1,0:T(8,128)} %get-tuple-element.12), channel_id=1, source_target_pairs={{1,0},{2,1},{3,2},{4,3},{5,4},{6,5},{7,6},{8,7},{9,8},{10,9},{11,1... | collective-permute-start | bytes 1179656 | tf_op jit(solution)/shard_map/ppermute | solution.py:148
Sparse Core Ops, SparseCore 0:
  44.2 95.1 all-reduce.2
  173.0 93.9 all-reduce.4

commit v2 on v1

--- a/solution.py
+++ b/solution.py
@@ -17,6 +17,9 @@
 PROPAGATION = 4.0
 DAMPING = 1.0
 TINY = 1e-06
+LANES = 128
+VMEM_LIMIT = 48 * 1024 * 1024
+MESH = pl.DeviceIdType.MESH
 
 
 def split_table(table):
@@ -67,14 +70,28 @@
     return a_re * b_re - a_im * b_im, a_re * b_im + a_im * b_re
 
 
+def joined(ref, plane, length):
+    rows = ref.shape[1]
+    return jnp.concatenate(
+        [ref[plane, start : start + length] for start in range(0, rows, length)], axis=1
+    )
+
+
 def local_kernel(
     rows_ref, cols_ref, first_ref, field, probe, intensity, dft_l, dft_r, spread_l, spread_r,
-    grad, sums, window,
+    grad, sums, loss, window,
 ):
-    length = probe.shape[1]
+    length = intensity.shape[1]
     width = field.shape[3]
     grad[...] = jnp.zeros_like(grad)
     sums[...] = jnp.zeros_like(sums)
+    loss[...] = jnp.zeros_like(loss)
+    light_re, light_im = joined(probe, 0, length), joined(probe, 1, length)
+
+    def collect(plane, value):
+        for part in range(length // LANES):
+            rows = pl.ds(part * length, length)
+            sums[plane, rows, :] += value[:, part * LANES : (part + 1) * LANES]
 
     @pl.loop(0, intensity.shape[0])
     def _(index):
@@ -93,24 +110,25 @@
         front_at = jnp.where(chosen, 0, 1)
         behind_at = 1 - front_at
         front_re, front_im = window[front_at, 0], window[front_at, 1]
-        wave_re, wave_im = times(probe[0], probe[1], front_re, front_im)
-        sums[2 * length : 3 * length] += front_re * front_re + front_im * front_im
+        wave_re, wave_im = times(light_re, light_im, front_re, front_im)
+        collect(2, front_re * front_re + front_im * front_im)
         near_re, near_im = both_sides(wave_re, wave_im, spread_l, spread_r)
         exit_re, exit_im = times(near_re, near_im, window[behind_at, 0], window[behind_at, 1])
         far_re, far_im = both_sides(exit_re, exit_im, dft_l, dft_r)
         modulus = jnp.sqrt(far_re * far_re + far_im * far_im + SMOOTHING)
         misfit = modulus - jnp.sqrt(intensity[index] + SMOOTHING)
-        squares = (misfit * misfit).reshape(length // 8, 8, length)
-        sums[3 * length : 3 * length + 8] += jnp.sum(squares, axis=0)
+        squares = jnp.sum((misfit * misfit).reshape(length // 8, 8, length), axis=0)
+        for part in range(length // LANES):
+            loss[...] += squares[:, part * LANES : (part + 1) * LANES]
         slope = 2.0 * misfit / modulus
         exit_re, exit_im = both_sides(slope * far_re, -slope * far_im, dft_l, dft_r)
         behind_re, behind_im = times(near_re, near_im, exit_re, exit_im)
         near_re, near_im = times(window[behind_at, 0], window[behind_at, 1], exit_re, exit_im)
         wave_re, wave_im = both_sides(near_re, near_im, spread_l, spread_r)
         probe_re, probe_im = times(window[front_at, 0], window[front_at, 1], wave_re, wave_im)
-        sums[:length] += probe_re
-        sums[length : 2 * length] -= probe_im
-        front_re, front_im = times(probe[0], probe[1], wave_re, wave_im)
+        collect(0, probe_re)
+        collect(1, -probe_im)
+        front_re, front_im = times(light_re, light_im, wave_re, wave_im)
         below = jnp.zeros((8, length), jnp.float32)
         beside = jnp.zeros((length + 8, width - length), jnp.float32)
         for which, part, value in (
@@ -125,62 +143,346 @@
 
 
 def local_terms(field, probe, intensity, rows, cols, first):
-    length = probe.shape[1]
+    length = intensity.shape[1]
     vmem = pl.BlockSpec(memory_space=pltpu.VMEM)
     smem = pl.BlockSpec(memory_space=pltpu.SMEM)
     return pl.pallas_call(
         local_kernel,
         out_shape=(
             jax.ShapeDtypeStruct(field.shape, jnp.float32),
-            jax.ShapeDtypeStruct((3 * length + 8, length), jnp.float32),
+            jax.ShapeDtypeStruct((3, length * length // LANES, LANES), jnp.float32),
+            jax.ShapeDtypeStruct((8, LANES), jnp.float32),
         ),
         in_specs=[smem] * 3 + [vmem] * 7,
-        out_specs=(vmem, vmem),
+        out_specs=(vmem,) * 3,
         scratch_shapes=[pltpu.VMEM((2, 2, length, length), jnp.float32)],
-        compiler_params=pltpu.CompilerParams(vmem_limit_bytes=48 * 1024 * 1024),
+        compiler_params=pltpu.CompilerParams(vmem_limit_bytes=VMEM_LIMIT),
     )(rows, cols, first, field, probe, intensity, *(jnp.asarray(t) for t in tables(length)))
 
 
-def from_sides(to_before, to_after):
+def greet(devices):
+    barrier = pltpu.get_barrier_semaphore()
+    for condition, device in devices:
+
+        @pl.when(condition)
+        def _(device=device):
+            pl.semaphore_signal(barrier, inc=1, device_id={"row": device}, device_id_type=MESH)
+
+    pl.semaphore_wait(barrier, sum(condition.astype(jnp.int32) for condition, _ in devices))
+
+
+def send(source, target, send_sem, recv_sem, device):
+    return pltpu.make_async_remote_copy(
+        src_ref=source,
+        dst_ref=target,
+        send_sem=send_sem,
+        recv_sem=recv_sem,
+        device_id={"row": device},
+        device_id_type=MESH,
+    )
+
+
+def first_kernel(devices, own, field, above, below, send_sem, recv_sem):
+    me = lax.axis_index("row")
+    tile = own.shape[2]
+    has_before, has_after = me > 0, me < devices - 1
+    greet(((has_before, me - 1), (has_after, me + 1)))
+    up = send(own.at[:, :, pl.ds(0, MARGIN)], below, send_sem.at[0], recv_sem.at[0], me - 1)
+    down = send(
+        own.at[:, :, pl.ds(tile - MARGIN, MARGIN)], above, send_sem.at[1], recv_sem.at[1], me + 1
+    )
+    pl.when(has_before)(up.start)
+    pl.when(has_after)(down.start)
+    field[:, :, MARGIN : MARGIN + tile] = own[...]
+
+    @pl.when(has_before)
+    def _():
+        down.wait_recv()
+        field[:, :, :MARGIN] = above[...]
+
+    @pl.when(me == 0)
+    def _():
+        field[:, :, :MARGIN] = jnp.zeros_like(above)
+
+    @pl.when(has_after)
+    def _():
+        up.wait_recv()
+        field[:, :, MARGIN + tile :] = below[...]
+
+    @pl.when(me == devices - 1)
+    def _():
+        field[:, :, MARGIN + tile :] = jnp.zeros_like(below)
+
+    pl.when(has_before)(up.wait_send)
+    pl.when(has_after)(down.wait_send)
+
+
+def first_field(own):
+    planes, parts, tile, width = own.shape
+    vmem = pl.BlockSpec(memory_space=pltpu.VMEM)
+    edge = pltpu.VMEM((planes, parts, MARGIN, width), jnp.float32)
+    return pl.pallas_call(
+        functools.partial(first_kernel, lax.axis_size("row")),
+        out_shape=jax.ShapeDtypeStruct((planes, parts, tile + 2 * MARGIN, width), jnp.float32),
+        in_specs=[vmem],
+        out_specs=vmem,
+        scratch_shapes=[edge, edge, pltpu.SemaphoreType.DMA((2,)), pltpu.SemaphoreType.DMA((2,))],
+        compiler_params=pltpu.CompilerParams(
+            collective_id=0, has_side_effects=True, vmem_limit_bytes=VMEM_LIMIT
+        ),
+    )(own)
+
+
+def renew_kernel(
+    devices, last, grad, sums, loss, field, probe, field_out, probe_out, loss_out,
+    from_pair, loss_pair, to_peer, from_peer, renewed, above, below,
+    pair_send, pair_recv, loss_sem, peer_send, peer_recv, spread_send, spread_recv,
+    back_send, back_recv, edge_send, edge_recv,
+):
+    me = lax.axis_index("row")
+    peers = devices // 2
+    core, place = lax.rem(me, 2), lax.div(me, 2)
+    partner = me + 1 - 2 * core
+    piece = sums.shape[1] // devices
+    extent, tile = field.shape[2], field.shape[2] - 2 * MARGIN
+    reach = above.shape[2]
+    has_before, has_after = me > 0, me < devices - 1
+
+    def rows_of(side, index):
+        return pl.ds(pl.multiple_of((side * peers + index) * piece, piece), piece)
+
+    def to_pair(index, side):
+        return send(
+            sums.at[:, rows_of(side, index)], from_pair.at[index],
+            pair_send.at[index], pair_recv.at[index], partner,
+        )
+
+    def to_place(index, slot):
+        return send(
+            to_peer.at[index], from_peer.at[slot],
+            peer_send.at[index], peer_recv.at[slot], 2 * index + core,
+        )
+
+    def spread(index, slot):
+        part = renewed.at[:, rows_of(core, slot)]
+        return send(part, part, spread_send.at[index], spread_recv.at[slot], 2 * index + core)
+
+    def back(index, side):
+        part = renewed.at[:, rows_of(side, index)]
+        return send(part, part, back_send.at[index], back_recv.at[index], partner)
+
+    def after_me(step):
+        return lax.rem(place + 1 + step, peers)
+
+    def before_me(step):
+        return lax.rem(place + peers - 1 - step, peers)
+
+    other = me - 1 + 2 * core
+    barrier = pltpu.get_barrier_semaphore()
+
+    def signal(device):
+        pl.semaphore_signal(barrier, inc=1, device_id={"row": device}, device_id_type=MESH)
+
+    signal(partner)
+
+    @pl.loop(0, peers - 1)
+    def _(step):
+        signal(2 * after_me(step) + core)
+
+    beside = (other >= 0) & (other < devices)
+
+    @pl.when(beside)
+    def _():
+        signal(other)
+
+    pl.semaphore_wait(barrier, peers + beside.astype(jnp.int32))
+
+    to_loss = send(loss, loss_pair, loss_sem.at[0], loss_sem.at[1], partner)
+    to_loss.start()
+
+    @pl.loop(0, peers)
+    def _(step):
+        to_pair(after_me(step), 1 - core).start()
+
+    up = send(grad.at[:, :, pl.ds(0, reach)], below, edge_send.at[0], edge_recv.at[0], me - 1)
+    down = send(
+        grad.at[:, :, pl.ds(extent - reach, reach)], above, edge_send.at[1], edge_recv.at[1], me + 1
+    )
+    pl.when(has_before)(up.start)
+    pl.when(has_after)(down.start)
+
+    to_loss.wait()
+    pair_loss = loss[...] + loss_pair[...]
+
+    def add_pair(index):
+        to_pair(index, core).wait_recv()
+        both = sums[:, rows_of(core, index), :] + from_pair[index]
+        return both
+
+    @pl.loop(0, peers - 1)
+    def _(step):
+        index = after_me(step)
+        both = add_pair(index)
+        for plane in range(3):
+            to_peer[index, plane * piece : (plane + 1) * piece] = both[plane]
+        to_peer[index, 3 * piece :] = pair_loss
+        to_place(index, place).start()
+
+    both = add_pair(place)
+    for plane in range(3):
+        from_peer[place, plane * piece : (plane + 1) * piece] = both[plane]
+    from_peer[place, 3 * piece :] = pair_loss
+
+    square = probe[0] * probe[0] + probe[1] * probe[1]
+    rate = OBJECT_RATE / (jnp.sum(square, keepdims=True) / (square.size) + TINY)
+
+    @pl.loop(0, peers - 1)
+    def _(step):
+        index = before_me(step)
+        to_place(index, index).wait_recv()
+
+    total = from_peer[0]
+    for index in range(1, peers):
+        total = total + from_peer[index]
+    loss_out[...] = total[3 * piece :]
+    mine = rows_of(core, place)
+    weight = total[2 * piece : 3 * piece] + DAMPING
+    for part in range(2):
+        step = PROBE_RATE * total[part * piece : (part + 1) * piece] / weight
+        renewed[part, mine, :] = probe[part, mine, :] - step
+
+    @pl.loop(0, peers - 1)
+    def _(step):
+        spread(after_me(step), place).start()
+
+    back(place, core).start()
+
+    first_row = MARGIN if last else 0
+    planes = [(which, part) for which in range(grad.shape[0]) for part in range(grad.shape[1])]
+    for which, part in planes:
+        low, high = reach + first_row, extent - reach - first_row
+        field_out[which, part, reach : high - first_row] = (
+            field[which, part, low:high] - rate * grad[which, part, low:high]
+        )
+
+    @pl.loop(0, peers - 1)
+    def _(step):
+        index = before_me(step)
+        spread(index, index).wait_recv()
+        back(index, core).start()
+
+    @pl.when(has_before)
+    def _():
+        down.wait_recv()
+
+    @pl.when(me == 0)
+    def _():
+        above[...] = jnp.zeros_like(above)
+
+    for which, part in planes:
+        rows = slice(first_row, first_row + reach)
+        field_out[which, part, :reach] = field[which, part, rows] - rate * (
+            grad[which, part, rows] + above[which, part]
+        )
+
+    @pl.when(has_after)
+    def _():
+        up.wait_recv()
+
+    @pl.when(me == devices - 1)
+    def _():
+        below[...] = jnp.zeros_like(below)
+
+    for which, part in planes:
+        rows = slice(extent - first_row - reach, extent - first_row)
+        field_out[which, part, extent - 2 * first_row - reach :] = field[which, part, rows] - rate * (
+            grad[which, part, rows] + below[which, part]
+        )
+
+    if not last:
+
+        @pl.when(me == 0)
+        def _():
+            field_out[:, :, :MARGIN] = jnp.zeros(field[:, :, :MARGIN].shape, jnp.float32)
+
+        @pl.when(me == devices - 1)
+        def _():
+            field_out[:, :, extent - MARGIN :] = jnp.zeros(field[:, :, :MARGIN].shape, jnp.float32)
+
+    @pl.loop(0, peers)
+    def _(index):
+        back(index, 1 - core).wait_recv()
+
+    probe_out[...] = renewed[...]
+
+    @pl.loop(0, peers)
+    def _(index):
+        to_pair(index, 1 - core).wait_send()
+        back(index, core).wait_send()
+
+    @pl.loop(0, peers - 1)
+    def _(step):
+        index = after_me(step)
+        to_place(index, place).wait_send()
+        spread(index, place).wait_send()
+
+    pl.when(has_before)(up.wait_send)
+    pl.when(has_after)(down.wait_send)
+
+
+def renew(grad, sums, loss, field, probe, last):
     devices = lax.axis_size("row")
-    up = [(i, i + 1) for i in range(devices - 1)]
-    down = [(i + 1, i) for i in range(devices - 1)]
-    return lax.ppermute(to_after, "row", up), lax.ppermute(to_before, "row", down)
+    peers = devices // 2
+    planes, parts, extent, width = field.shape
+    piece = sums.shape[1] // devices
+    reach = MARGIN if last else 2 * MARGIN
+    height = extent - 2 * MARGIN if last else extent
+    vmem = pl.BlockSpec(memory_space=pltpu.VMEM)
+    edge = pltpu.VMEM((planes, parts, reach, width), jnp.float32)
+    packet = pltpu.VMEM((peers, 3 * piece + 8, LANES), jnp.float32)
+    each = pltpu.SemaphoreType.DMA((peers,))
+    two = pltpu.SemaphoreType.DMA((2,))
+    return pl.pallas_call(
+        functools.partial(renew_kernel, devices, last),
+        out_shape=(
+            jax.ShapeDtypeStruct((planes, parts, height, width), jnp.float32),
+            jax.ShapeDtypeStruct(probe.shape, jnp.float32),
+            jax.ShapeDtypeStruct(loss.shape, jnp.float32),
+        ),
+        in_specs=[vmem] * 5,
+        out_specs=(vmem,) * 3,
+        scratch_shapes=[
+            pltpu.VMEM((peers, 3, piece, LANES), jnp.float32),
+            pltpu.VMEM(loss.shape, jnp.float32),
+            packet,
+            packet,
+            pltpu.VMEM(probe.shape, jnp.float32),
+            edge,
+            edge,
+            each, each, two, each, each, each, each, each, each, two, two,
+        ],
+        compiler_params=pltpu.CompilerParams(
+            collective_id=2 if last else 1, has_side_effects=True, vmem_limit_bytes=VMEM_LIMIT
+        ),
+    )(grad, sums, loss, field, probe)
 
 
 def shards(object_field, probe, intensity, row_offset, col_offset, slice_first):
     length = probe.shape[1]
-    tile = object_field.shape[2]
+    parts = length // LANES
     count = intensity.shape[0] * lax.axis_size("row") * length * length
-    before, after = from_sides(object_field[:, :, :MARGIN], object_field[:, :, tile - MARGIN :])
-    field = jnp.concatenate([before, object_field, after], axis=2)
-    here = lax.axis_index("row")
-    inside = jnp.arange(tile + 2 * MARGIN)[:, None]
-    inside = ((inside >= MARGIN) | (here > 0)) & (
-        (inside < tile + MARGIN) | (here < lax.axis_size("row") - 1)
-    )
+    light = probe.reshape(2, length, parts, LANES).transpose(0, 2, 1, 3)
+    light = light.reshape(2, parts * length, LANES)
+    field = first_field(object_field)
     losses = []
     for step in range(ITERS):
-        grad, sums = local_terms(field, probe, intensity, row_offset, col_offset, slice_first)
-        rate = OBJECT_RATE / (jnp.mean(probe[0] * probe[0] + probe[1] * probe[1]) + TINY)
-        sums = lax.psum(sums, "row")
-        if step < ITERS - 1:
-            before, after = from_sides(grad[:, :, : 2 * MARGIN], grad[:, :, tile:])
-            middle = jnp.zeros_like(grad[:, :, : tile - 2 * MARGIN])
-            grad = grad + jnp.concatenate([before, middle, after], axis=2)
-            field = jnp.where(inside, field - rate * grad, 0.0)
-        else:
-            before, after = from_sides(grad[:, :, :MARGIN], grad[:, :, tile + MARGIN :])
-            middle = jnp.zeros_like(grad[:, :, : tile - 2 * MARGIN])
-            grad = grad[:, :, MARGIN : tile + MARGIN] + jnp.concatenate(
-                [before, middle, after], axis=2
-            )
-            field = field[:, :, MARGIN : tile + MARGIN] - rate * grad
-        summed = sums[: 2 * length].reshape(2, length, length)
-        weight = sums[2 * length : 3 * length]
-        probe = probe - PROBE_RATE * summed / (weight + DAMPING)
-        losses.append(jnp.sum(sums[3 * length :]) / count)
-    return field, probe, jnp.stack(losses)
+        grad, sums, loss = local_terms(
+            field, light, intensity, row_offset, col_offset, slice_first
+        )
+        field, light, loss = renew(grad, sums, loss, field, light, step == ITERS - 1)
+        losses.append(jnp.sum(loss) / count)
+    light = light.reshape(2, parts, length, LANES).transpose(0, 2, 1, 3)
+    return field, light.reshape(probe.shape), jnp.stack(losses)
 
 
 def solution(mesh):

time: 280 us -> 134 us (0.48)
  waiting for transfers between devices: 183 us -> 0 us
  Pallas kernels: 38.7 us -> 113 us
  starting transfers between devices: 16.5 us -> 0 us
  between operations: 17 us -> 2.05 us
  other arithmetic: 16.1 us -> 1.78 us
  local copies, waits for them, and re-layouts: 8.46 us -> 15.5 us
    psum x2 -> x0, waiting for transfers between devices: 172 us -> none  [shards(): sums = lax.psum(sums, 'row')]
    pallas_call x0 -> x3, Pallas kernels: none -> 75.1 us  [the longest x2 63.5 us: renew(): pl.pallas_call(functools.partial(renew_kernel, devices, last), out_shape=...]
    ppermute x6 -> x0, starting transfers between devices: 16.4 us -> none  [the longest x3 8.61 us: from_sides(): lax.ppermute(to_after, 'row', up)]
    unnamed x28 -> x31, local copies, waits for them, and re-layouts: 2.29 us -> 13.6 us
    ppermute x6 -> x0, waiting for transfers between devices: 10.9 us -> none  [the longest x3 8.49 us: from_sides(): lax.ppermute(to_before, 'row', down)]
    slice x3 -> x0, local copies, waits for them, and re-layouts: 6.11 us -> none  [the longest x1 2.63 us: shards(): before, after = from_sides(grad[:, :, :2 * MARGIN], grad[:, :, tile:])]
    select_n x1 -> x0, other arithmetic: 3.76 us -> none  [shards(): field = jnp.where(inside, field - rate * grad, 0.0)]
    sub x3 -> x0, other arithmetic: 3.58 us -> none  [the longest x1 2.62 us: shards(): field = field[:, :, MARGIN:tile + MARGIN] - rate * grad]
  transfers between devices with their start and end apart: 8 -> 0, of which waited for: 5 -> 0; matrix products, arithmetic and copies ran while one was open for 4% -> 0% of each run, Pallas kernels for 0% -> 0%
where the time goes in v2:
time: 134 us; the launch traced here: 133 us
  Pallas kernels  113 us (84%)
  local copies, waits for them, and re-layouts  15.5 us (12%)
  between operations  2.05 us (2%)
  other arithmetic  1.78 us (1%)
    pallas_call x2, Pallas kernels, renew(): pl.pallas_call(functools.partial(renew_kernel, devices, last), out_shape=...  63.5 us
    pallas_call x2, Pallas kernels, local_terms(): pl.pallas_call(local_kernel, out_shape=(jax.ShapeDtypeStruct(field.shape,...  38.3 us
    unnamed x31, local copies, waits for them, and re-layouts  13.6 us
    pallas_call x1, Pallas kernels, first_field(): pl.pallas_call(functools.partial(first_kernel, lax.axis_size('row')), out...  11.6 us

profile of v2, /device:TPU:1, one launch (start us, length us, event | category | flops | bytes accessed | tf_op | source)
XLA Modules:
  0.0 132.8 jit_solution(14249553183604759922)
XLA Ops:
  0.6 0.0 copy-start
  0.6 1.0 copy-done
  1.7 0.0 copy-start.6
  1.7 0.0 copy-start.12
  1.7 0.0 copy-start.13
  1.7 0.0 copy-start.14
  1.7 0.0 copy-start.9
  1.7 1.3 copy-done.9
  3.1 0.0 copy-start.3
  3.1 0.0 copy-start.4
  3.1 11.6 %shard_map.121.field = f32[2,2,320,384]{3,2,1,0:T(8,128)S(1)} custom-call(f32[2,2,192,384]{3,2,1,0:T(8,128)S(1)} %copy-done.9), custom_call_target="tpu_custom_call" | custom-call | tf_op jit(solution)/shard_map/pallas_call | solution.py:224
  14.7 0.0 copy-start.1
  14.7 1.3 copy-done.1
  16.0 0.0 copy-done.6
  16.0 0.0 copy-done.12
  16.0 0.0 copy-done.13
  16.0 0.0 copy-done.14
  16.0 0.0 copy-done.3
  16.0 0.0 copy-done.4
  16.0 19.1 %shard_map.122 = (f32[2,2,320,384]{3,2,1,0:T(8,128)}, f32[3,512,128]{2,1,0:T(8,128)S(1)}, f32[8,128]{1,0:T(8,128)S(1)}) custom-call(s32[2]{0:T(128)S(1)} %copy-done.12, s32[2]{0:T(128)S(1)} %copy-done.13, s32[2]{0:T(128)S(1)} %copy-done.14, f32[2,2,320,384]{3,2,1,0:T(8,128)} %copy-done.1, f32[2,512,128]{2,1,0:T(8,128)S(1)} %bitcast.17, ...), custom_call_target="tpu_custom_call" | custom-call | tf_op jit(solution)/shard_map/pallas_call | solution.py:149
  35.1 0.0 copy-start.8
  35.1 1.5 %copy-done.8 = f32[2,2,320,384]{3,2,1,0:T(8,128)S(1)} copy-done((f32[2,2,320,384]{3,2,1,0:T(8,128)S(1)}, f32[2,2,320,384]{3,2,1,0:T(8,128)}, u32[]{:S(2)}) %copy-start.8) | copy-done | bytes 1966104
  36.7 35.9 %shard_map.123 = (f32[2,2,320,384]{3,2,1,0:T(8,128)S(1)}, f32[2,512,128]{2,1,0:T(8,128)S(1)}, f32[8,128]{1,0:T(8,128)S(1)}) custom-call(f32[2,2,320,384]{3,2,1,0:T(8,128)S(1)} %copy-done.8, f32[3,512,128]{2,1,0:T(8,128)S(1)} %get-tuple-element.16.sums, f32[8,128]{1,0:T(8,128)S(1)} %get-tuple-element.17.loss, f32[2,2,320,384]{3,2,1,0:T(8,128)} %copy-done.1, ...), custom_call_target="tpu_custom_call" | custom-call | tf_op jit(solution)/shard_map/pallas_call | solution.py:445
  72.5 0.0 copy-start.2
  72.5 1.3 copy-done.2
  73.8 0.6 reduce_sum.18
  75.1 0.0 copy-start.5
  75.1 1.4 %copy-done.5 = bf16[512,1536]{1,0:T(8,128)(2,1)S(1)} copy-done((bf16[512,1536]{1,0:T(8,128)(2,1)S(1)}, bf16[512,1536]{1,0:T(8,128)(2,1)}, u32[]{:S(2)}) %copy-start.5) | copy-done | bytes 1572888
  76.5 19.2 %shard_map.124 = (f32[2,2,320,384]{3,2,1,0:T(8,128)}, f32[3,512,128]{2,1,0:T(8,128)S(1)}, f32[8,128]{1,0:T(8,128)S(1)}) custom-call(s32[2]{0:T(128)S(1)} %copy-done.12, s32[2]{0:T(128)S(1)} %copy-done.13, s32[2]{0:T(128)S(1)} %copy-done.14, f32[2,2,320,384]{3,2,1,0:T(8,128)} %copy-done.2, f32[2,512,128]{2,1,0:T(8,128)S(1)} %get-tuple-element.19.probe, ...), custom_call_target="tpu_custom_call" | custom-call | tf_op jit(solution)/shard_map/pallas_call | solution.py:149
  95.7 0.0 copy-start.7
  95.7 1.5 %copy-done.7 = f32[2,2,320,384]{3,2,1,0:T(8,128)S(1)} copy-done((f32[2,2,320,384]{3,2,1,0:T(8,128)S(1)}, f32[2,2,320,384]{3,2,1,0:T(8,128)}, u32[]{:S(2)}) %copy-start.7) | copy-done | bytes 1966104
  97.2 27.6 %shard_map.125 = (f32[2,2,192,384]{3,2,1,0:T(8,128)S(1)}, f32[2,512,128]{2,1,0:T(8,128)S(1)}, f32[8,128]{1,0:T(8,128)S(1)}) custom-call(f32[2,2,320,384]{3,2,1,0:T(8,128)S(1)} %copy-done.7, f32[3,512,128]{2,1,0:T(8,128)S(1)} %get-tuple-element.21.sums, f32[8,128]{1,0:T(8,128)S(1)} %get-tuple-element.22.loss, f32[2,2,320,384]{3,2,1,0:T(8,128)} %copy-done.2, ...), custom_call_target="tpu_custom_call" | custom-call | tf_op jit(solution)/shard_map/pallas_call | solution.py:445
  124.9 0.0 copy-start.10
  124.9 1.0 copy-done.10
  125.9 0.0 copy-start.11
  125.9 0.8 copy-done.11
  126.7 0.6 reduce_sum.19
  127.9 0.6 pad_maximum_fusion
  128.5 1.9 %copy.19 = f32[2,2,32,8,128]{4,3,1,2,0:T(8,128)} copy(f32[2,2,32,8,128]{4,3,2,1,0:T(8,128)} %bitcast.19) | data formatting | bytes 1048576 | tf_op jit(solution)/shard_map/reshape | solution.py:485
  130.4 2.4 %copy.21 = f32[2,2,192,384]{3,2,1,0:T(8,128)} copy(f32[2,2,192,384]{3,2,1,0:T(8,128)} %copy-done.10) | data formatting | bytes 2359296
  (1 shorter events, 0.0 us)
Async XLA Ops:
  0.6 1.0 copy-start
  1.7 14.3 %copy-start.6 = (f32[2,256,256]{2,1,0:T(8,128)S(1)}, f32[2,256,256]{2,1,0:T(8,128)}, u32[]{:S(2)}) copy-start(f32[2,256,256]{2,1,0:T(8,128)} %intensity.3) | copy-start | bytes 1572868
  1.7 14.3 %copy-start.12 = (s32[2]{0:T(128)S(1)}, s32[2]{0:T(128)}, u32[]{:S(2)}) copy-start(s32[2]{0:T(128)} %rows_ref.3) | copy-start | bytes 28
  1.7 14.3 %copy-start.13 = (s32[2]{0:T(128)S(1)}, s32[2]{0:T(128)}, u32[]{:S(2)}) copy-start(s32[2]{0:T(128)} %cols_ref.3) | copy-start | bytes 28
  1.7 14.3 %copy-start.14 = (s32[2]{0:T(128)S(1)}, s32[2]{0:T(128)}, u32[]{:S(2)}) copy-start(s32[2]{0:T(128)} %first_ref.3) | copy-start | bytes 28
  1.7 1.3 copy-start.9
  3.1 12.9 %copy-start.3 = (bf16[1536,512]{1,0:T(8,128)(2,1)S(1)}, bf16[1536,512]{1,0:T(8,128)(2,1)}, u32[]{:S(2)}) copy-start(bf16[1536,512]{1,0:T(8,128)(2,1)} %constant.15.clone.dft_r) | copy-start | bytes 4718596
  3.1 12.9 %copy-start.4 = (bf16[512,1536]{1,0:T(8,128)(2,1)S(1)}, bf16[512,1536]{1,0:T(8,128)(2,1)}, u32[]{:S(2)}) copy-start(bf16[512,1536]{1,0:T(8,128)(2,1)} %constant.14.clone.dft_l) | copy-start | bytes 4718596
  14.7 1.3 copy-start.1
  35.1 1.5 %copy-start.8 = (f32[2,2,320,384]{3,2,1,0:T(8,128)S(1)}, f32[2,2,320,384]{3,2,1,0:T(8,128)}, u32[]{:S(2)}) copy-start(f32[2,2,320,384]{3,2,1,0:T(8,128)} %get-tuple-element.15.grad) | copy-start | bytes 5898244
  72.5 1.3 copy-start.2
  75.1 1.4 %copy-start.5 = (bf16[512,1536]{1,0:T(8,128)(2,1)S(1)}, bf16[512,1536]{1,0:T(8,128)(2,1)}, u32[]{:S(2)}) copy-start(bf16[512,1536]{1,0:T(8,128)(2,1)} %constant.14.clone.dft_l) | copy-start | bytes 4718596
  95.7 1.5 %copy-start.7 = (f32[2,2,320,384]{3,2,1,0:T(8,128)S(1)}, f32[2,2,320,384]{3,2,1,0:T(8,128)}, u32[]{:S(2)}) copy-start(f32[2,2,320,384]{3,2,1,0:T(8,128)} %get-tuple-element.20.grad) | copy-start | bytes 5898244
  124.9 1.0 copy-start.10
  125.9 0.8 copy-start.11

commit v3 on v2

--- a/solution.py
+++ b/solution.py
@@ -18,6 +18,7 @@
 DAMPING = 1.0
 TINY = 1e-06
 LANES = 128
+STRIP = 32
 VMEM_LIMIT = 48 * 1024 * 1024
 MESH = pl.DeviceIdType.MESH
 
@@ -42,108 +43,149 @@
     return split_table(dft) + split_table(spread)
 
 
-def halves(value):
-    high = value.astype(jnp.bfloat16)
-    low = (value - high.astype(jnp.float32)).astype(jnp.bfloat16)
-    return high, low
-
-
-def both_sides(re, im, on_left, on_right):
-    length = re.shape[0]
-    high, low = halves(jnp.concatenate([re, im], axis=1))
-    rows = jnp.dot(
-        jnp.concatenate([high, low, high], axis=1),
-        on_right[...],
-        preferred_element_type=jnp.float32,
-    )
-    stacked = jnp.concatenate([rows[:, :length], rows[:, length:]], axis=0)
-    high, low = halves(stacked)
-    done = jnp.dot(
-        on_left[...],
-        jnp.concatenate([high, high, low], axis=0),
-        preferred_element_type=jnp.float32,
-    )
-    return done[:length], done[length:]
+def joined(ref, plane, rows, length):
+    return jnp.concatenate(
+        [ref[plane, start + rows.start : start + rows.stop] for start in range(0, ref.shape[1], length)],
+        axis=1,
+    )
 
 
 def times(a_re, a_im, b_re, b_im):
     return a_re * b_re - a_im * b_im, a_re * b_im + a_im * b_re
 
 
-def joined(ref, plane, length):
-    rows = ref.shape[1]
-    return jnp.concatenate(
-        [ref[plane, start : start + length] for start in range(0, rows, length)], axis=1
-    )
-
-
 def local_kernel(
     rows_ref, cols_ref, first_ref, field, probe, intensity, dft_l, dft_r, spread_l, spread_r,
-    grad, sums, loss, window,
+    grad, sums, loss, window, on_left, on_right, between, after, near,
 ):
-    length = intensity.shape[1]
-    width = field.shape[3]
+    count, length = intensity.shape[:2]
+    tiles = field.shape[2]
+    strips = [slice(start, start + STRIP) for start in range(0, length, STRIP)]
+    lane = lax.broadcasted_iota(jnp.int32, (STRIP, LANES), 1)
+    row_at = [rows_ref[index] for index in range(count)]
+    col_at = [cols_ref[index] for index in range(count)]
+    front_at = [first_ref[index] for index in range(count)]
+
+    def columns(index):
+        return slice(index * length, (index + 1) * length)
+
+    def set_left(index, rows, re, im):
+        at = slice(index * length + rows.start, index * length + rows.stop)
+        for value, start in ((re, 0), (im, length)):
+            high = value.astype(jnp.bfloat16)
+            low = (value - high.astype(jnp.float32)).astype(jnp.bfloat16)
+            on_left[at, start : start + length] = high
+            on_left[at, start + 2 * length : start + 3 * length] = low
+            on_left[at, start + 4 * length : start + 5 * length] = high
+
+    def both_sides(table_l, table_r):
+        between[...] = jnp.dot(on_left[...], table_r[...], preferred_element_type=jnp.float32)
+        for index in range(count):
+            for rows in strips:
+                at = slice(index * length + rows.start, index * length + rows.stop)
+                for start in (0, length):
+                    value = between[at, start : start + length]
+                    high = value.astype(jnp.bfloat16)
+                    low = (value - high.astype(jnp.float32)).astype(jnp.bfloat16)
+                    for base, piece in ((0, high), (2 * length, high), (4 * length, low)):
+                        first = base + start + rows.start
+                        on_right[first : first + STRIP, columns(index)] = piece
+        after[...] = jnp.dot(table_l[...], on_right[...], preferred_element_type=jnp.float32)
+
+    def result(index, rows):
+        below = slice(length + rows.start, length + rows.stop)
+        return after[rows, columns(index)], after[below, columns(index)]
+
     grad[...] = jnp.zeros_like(grad)
-    sums[...] = jnp.zeros_like(sums)
-    loss[...] = jnp.zeros_like(loss)
-    light_re, light_im = joined(probe, 0, length), joined(probe, 1, length)
-
-    def collect(plane, value):
-        for part in range(length // LANES):
-            rows = pl.ds(part * length, length)
-            sums[plane, rows, :] += value[:, part * LANES : (part + 1) * LANES]
-
-    @pl.loop(0, intensity.shape[0])
-    def _(index):
-        row = rows_ref[index]
-        col = cols_ref[index]
-        base = pl.multiple_of(jnp.minimum(row // 8 * 8, field.shape[2] - length - 8), 8)
-        extra = row - base
-        up = lax.rem(length + 8 - extra, length + 8)
-        taken = pl.ds(base, length + 8)
-        chosen = first_ref[index] == 0
-        back = lax.rem(width - col, width)
-        for which in range(2):
-            for part in range(2):
-                wide = pltpu.roll(field[which, part, taken, :], back, 1)[:, :length]
-                window[which, part] = pltpu.roll(wide, up, 0)[:length]
-        front_at = jnp.where(chosen, 0, 1)
-        behind_at = 1 - front_at
-        front_re, front_im = window[front_at, 0], window[front_at, 1]
-        wave_re, wave_im = times(light_re, light_im, front_re, front_im)
-        collect(2, front_re * front_re + front_im * front_im)
-        near_re, near_im = both_sides(wave_re, wave_im, spread_l, spread_r)
-        exit_re, exit_im = times(near_re, near_im, window[behind_at, 0], window[behind_at, 1])
-        far_re, far_im = both_sides(exit_re, exit_im, dft_l, dft_r)
-        modulus = jnp.sqrt(far_re * far_re + far_im * far_im + SMOOTHING)
-        misfit = modulus - jnp.sqrt(intensity[index] + SMOOTHING)
-        squares = jnp.sum((misfit * misfit).reshape(length // 8, 8, length), axis=0)
-        for part in range(length // LANES):
-            loss[...] += squares[:, part * LANES : (part + 1) * LANES]
-        slope = 2.0 * misfit / modulus
-        exit_re, exit_im = both_sides(slope * far_re, -slope * far_im, dft_l, dft_r)
-        behind_re, behind_im = times(near_re, near_im, exit_re, exit_im)
-        near_re, near_im = times(window[behind_at, 0], window[behind_at, 1], exit_re, exit_im)
-        wave_re, wave_im = both_sides(near_re, near_im, spread_l, spread_r)
-        probe_re, probe_im = times(window[front_at, 0], window[front_at, 1], wave_re, wave_im)
-        collect(0, probe_re)
-        collect(1, -probe_im)
-        front_re, front_im = times(light_re, light_im, wave_re, wave_im)
-        below = jnp.zeros((8, length), jnp.float32)
-        beside = jnp.zeros((length + 8, width - length), jnp.float32)
-        for which, part, value in (
-            (front_at, 0, front_re),
-            (front_at, 1, -front_im),
-            (behind_at, 0, behind_re),
-            (behind_at, 1, -behind_im),
-        ):
-            value = pltpu.roll(jnp.concatenate([value, below], axis=0), extra, 0)
-            wide = pltpu.roll(jnp.concatenate([value, beside], axis=1), col, 1)
-            grad[which, part, taken, :] += wide
+    for index in range(count):
+        back = lax.rem(LANES - col_at[index], LANES)
+        stays = lane < LANES - col_at[index]
+        for rows in strips:
+            taken = pl.ds(row_at[index] + rows.start, STRIP)
+            for which, source in ((0, front_at[index]), (1, 1 - front_at[index])):
+                for part in range(2):
+                    rolled = [
+                        pltpu.roll(field[source, part, tile, taken, :], back, 1)
+                        for tile in range(tiles)
+                    ]
+                    for tile in range(tiles - 1):
+                        window[index, which, part, rows, tile * LANES : (tile + 1) * LANES] = (
+                            jnp.where(stays, rolled[tile], rolled[tile + 1])
+                        )
+            front_re, front_im = window[index, 0, 0, rows], window[index, 0, 1, rows]
+            light_re, light_im = joined(probe, 0, rows, length), joined(probe, 1, rows, length)
+            set_left(index, rows, *times(light_re, light_im, front_re, front_im))
+
+    both_sides(spread_l, spread_r)
+    for index in range(count):
+        for rows in strips:
+            near_re, near_im = result(index, rows)
+            near[index, 0, rows] = near_re
+            near[index, 1, rows] = near_im
+            behind_re, behind_im = window[index, 1, 0, rows], window[index, 1, 1, rows]
+            set_left(index, rows, *times(near_re, near_im, behind_re, behind_im))
+
+    both_sides(dft_l, dft_r)
+    total = jnp.zeros((8, length), jnp.float32)
+    for index in range(count):
+        for rows in strips:
+            far_re, far_im = result(index, rows)
+            power = far_re * far_re + far_im * far_im + SMOOTHING
+            modulus = jnp.sqrt(power)
+            misfit = modulus - jnp.sqrt(intensity[index, rows] + SMOOTHING)
+            total += jnp.sum((misfit * misfit).reshape(STRIP // 8, 8, length), axis=0)
+            slope = 2.0 * misfit / modulus
+            set_left(index, rows, slope * far_re, -slope * far_im)
+    loss[...] = sum(
+        total[:, start : start + LANES] for start in range(0, length, LANES)
+    )
+
+    def scatter(index, rows, source, part, value):
+        col = lax.rem(col_at[index], LANES)
+        moved = lane < col_at[index]
+        taken = pl.ds(row_at[index] + rows.start, STRIP)
+        rolled = [
+            pltpu.roll(value[:, tile * LANES : (tile + 1) * LANES], col, 1)
+            for tile in range(tiles - 1)
+        ]
+        zero = jnp.zeros_like(rolled[0])
+        for tile in range(tiles):
+            here = rolled[tile] if tile < tiles - 1 else zero
+            ahead = rolled[tile - 1] if tile else zero
+            grad[source, part, tile, taken, :] += jnp.where(moved, ahead, here)
+
+    both_sides(dft_l, dft_r)
+    for index in range(count):
+        for rows in strips:
+            exit_re, exit_im = result(index, rows)
+            behind_re, behind_im = window[index, 1, 0, rows], window[index, 1, 1, rows]
+            set_left(index, rows, *times(behind_re, behind_im, exit_re, exit_im))
+            grad_re, grad_im = times(near[index, 0, rows], near[index, 1, rows], exit_re, exit_im)
+            scatter(index, rows, 1 - front_at[index], 0, grad_re)
+            scatter(index, rows, 1 - front_at[index], 1, -grad_im)
+
+    both_sides(spread_l, spread_r)
+    for rows in strips:
+        light_re, light_im = joined(probe, 0, rows, length), joined(probe, 1, rows, length)
+        planes = [jnp.zeros((STRIP, length), jnp.float32)] * 3
+        for index in range(count):
+            wave_re, wave_im = result(index, rows)
+            front_re, front_im = window[index, 0, 0, rows], window[index, 0, 1, rows]
+            probe_re, probe_im = times(front_re, front_im, wave_re, wave_im)
+            planes[0] += probe_re
+            planes[1] -= probe_im
+            planes[2] += front_re * front_re + front_im * front_im
+            grad_re, grad_im = times(light_re, light_im, wave_re, wave_im)
+            scatter(index, rows, front_at[index], 0, grad_re)
+            scatter(index, rows, front_at[index], 1, -grad_im)
+        for plane, value in enumerate(planes):
+            for part in range(length // LANES):
+                at = slice(part * length + rows.start, part * length + rows.stop)
+                sums[plane, at] = value[:, part * LANES : (part + 1) * LANES]
 
 
 def local_terms(field, probe, intensity, rows, cols, first):
-    length = intensity.shape[1]
+    count, length = intensity.shape[:2]
     vmem = pl.BlockSpec(memory_space=pltpu.VMEM)
     smem = pl.BlockSpec(memory_space=pltpu.SMEM)
     return pl.pallas_call(
@@ -155,7 +197,14 @@
         ),
         in_specs=[smem] * 3 + [vmem] * 7,
         out_specs=(vmem,) * 3,
-        scratch_shapes=[pltpu.VMEM((2, 2, length, length), jnp.float32)],
+        scratch_shapes=[
+            pltpu.VMEM((count, 2, 2, length, length), jnp.float32),
+            pltpu.VMEM((count * length, 6 * length), jnp.bfloat16),
+            pltpu.VMEM((6 * length, count * length), jnp.bfloat16),
+            pltpu.VMEM((count * length, 2 * length), jnp.float32),
+            pltpu.VMEM((2 * length, count * length), jnp.float32),
+            pltpu.VMEM((count, 2, length, length), jnp.float32),
+        ],
         compiler_params=pltpu.CompilerParams(vmem_limit_bytes=VMEM_LIMIT),
     )(rows, cols, first, field, probe, intensity, *(jnp.asarray(t) for t in tables(length)))
 
@@ -193,25 +242,35 @@
     )
     pl.when(has_before)(up.start)
     pl.when(has_after)(down.start)
-    field[:, :, MARGIN : MARGIN + tile] = own[...]
+
+    def place(start, rows, source):
+        for index in range(field.shape[2]):
+            columns = slice(index * LANES, (index + 1) * LANES)
+            field[:, :, index, start : start + rows] = (
+                jnp.zeros((2, 2, rows, LANES), jnp.float32)
+                if source is None
+                else source[:, :, :, columns]
+            )
+
+    place(MARGIN, tile, own)
 
     @pl.when(has_before)
     def _():
         down.wait_recv()
-        field[:, :, :MARGIN] = above[...]
+        place(0, MARGIN, above)
 
     @pl.when(me == 0)
     def _():
-        field[:, :, :MARGIN] = jnp.zeros_like(above)
+        place(0, MARGIN, None)
 
     @pl.when(has_after)
     def _():
         up.wait_recv()
-        field[:, :, MARGIN + tile :] = below[...]
+        place(MARGIN + tile, MARGIN, below)
 
     @pl.when(me == devices - 1)
     def _():
-        field[:, :, MARGIN + tile :] = jnp.zeros_like(below)
+        place(MARGIN + tile, MARGIN, None)
 
     pl.when(has_before)(up.wait_send)
     pl.when(has_after)(down.wait_send)
@@ -223,7 +282,9 @@
     edge = pltpu.VMEM((planes, parts, MARGIN, width), jnp.float32)
     return pl.pallas_call(
         functools.partial(first_kernel, lax.axis_size("row")),
-        out_shape=jax.ShapeDtypeStruct((planes, parts, tile + 2 * MARGIN, width), jnp.float32),
+        out_shape=jax.ShapeDtypeStruct(
+            (planes, parts, width // LANES, tile + 2 * MARGIN, LANES), jnp.float32
+        ),
         in_specs=[vmem],
         out_specs=vmem,
         scratch_shapes=[edge, edge, pltpu.SemaphoreType.DMA((2,)), pltpu.SemaphoreType.DMA((2,))],
@@ -244,8 +305,8 @@
     core, place = lax.rem(me, 2), lax.div(me, 2)
     partner = me + 1 - 2 * core
     piece = sums.shape[1] // devices
-    extent, tile = field.shape[2], field.shape[2] - 2 * MARGIN
-    reach = above.shape[2]
+    extent = field.shape[3]
+    reach = above.shape[3]
     has_before, has_after = me > 0, me < devices - 1
 
     def rows_of(side, index):
@@ -304,12 +365,12 @@
     def _(step):
         to_pair(after_me(step), 1 - core).start()
 
-    up = send(grad.at[:, :, pl.ds(0, reach)], below, edge_send.at[0], edge_recv.at[0], me - 1)
+    up = send(grad.at[:, :, :, pl.ds(0, reach)], below, edge_send.at[0], edge_recv.at[0], me - 1)
     down = send(
-        grad.at[:, :, pl.ds(extent - reach, reach)], above, edge_send.at[1], edge_recv.at[1], me + 1
-    )
-    pl.when(has_before)(up.start)
-    pl.when(has_after)(down.start)
+        grad.at[:, :, :, pl.ds(extent - reach, reach)], above, edge_send.at[1], edge_recv.at[1], me + 1
+    )
+    pl.when(core == 1)(up.start)
+    pl.when(core == 0)(down.start)
 
     to_loss.wait()
     pair_loss = loss[...] + loss_pair[...]
@@ -356,14 +417,29 @@
         spread(after_me(step), place).start()
 
     back(place, core).start()
+    pl.when((core == 0) & has_before)(up.start)
+    pl.when((core == 1) & has_after)(down.start)
 
     first_row = MARGIN if last else 0
-    planes = [(which, part) for which in range(grad.shape[0]) for part in range(grad.shape[1])]
-    for which, part in planes:
-        low, high = reach + first_row, extent - reach - first_row
-        field_out[which, part, reach : high - first_row] = (
-            field[which, part, low:high] - rate * grad[which, part, low:high]
-        )
+    planes = [
+        (which, part, index)
+        for which in range(grad.shape[0])
+        for part in range(grad.shape[1])
+        for index in range(grad.shape[2])
+    ]
+
+    def put(plane, start, value):
+        rows = slice(start, start + value.shape[0])
+        if last:
+            which, part, index = plane
+            field_out[which, part, rows, index * LANES : (index + 1) * LANES] = value
+        else:
+            field_out[(*plane, rows)] = value
+
+    low, high = reach + first_row, extent - reach - first_row
+    for plane in planes:
+        rows = (*plane, slice(low, high))
+        put(plane, reach, field[rows] - rate * grad[rows])
 
     @pl.loop(0, peers - 1)
     def _(step):
@@ -379,11 +455,9 @@
     def _():
         above[...] = jnp.zeros_like(above)
 
-    for which, part in planes:
-        rows = slice(first_row, first_row + reach)
-        field_out[which, part, :reach] = field[which, part, rows] - rate * (
-            grad[which, part, rows] + above[which, part]
-        )
+    for plane in planes:
+        rows = (*plane, slice(first_row, first_row + reach))
+        put(plane, 0, field[rows] - rate * (grad[rows] + above[plane]))
 
     @pl.when(has_after)
     def _():
@@ -393,21 +467,21 @@
     def _():
         below[...] = jnp.zeros_like(below)
 
-    for which, part in planes:
-        rows = slice(extent - first_row - reach, extent - first_row)
-        field_out[which, part, extent - 2 * first_row - reach :] = field[which, part, rows] - rate * (
-            grad[which, part, rows] + below[which, part]
-        )
+    for plane in planes:
+        rows = (*plane, slice(extent - first_row - reach, extent - first_row))
+        put(plane, extent - 2 * first_row - reach, field[rows] - rate * (grad[rows] + below[plane]))
 
     if not last:
 
         @pl.when(me == 0)
         def _():
-            field_out[:, :, :MARGIN] = jnp.zeros(field[:, :, :MARGIN].shape, jnp.float32)
+            field_out[:, :, :, :MARGIN] = jnp.zeros((*field.shape[:3], MARGIN, LANES), jnp.float32)
 
         @pl.when(me == devices - 1)
         def _():
-            field_out[:, :, extent - MARGIN :] = jnp.zeros(field[:, :, :MARGIN].shape, jnp.float32)
+            field_out[:, :, :, extent - MARGIN :] = jnp.zeros(
+                (*field.shape[:3], MARGIN, LANES), jnp.float32
+            )
 
     @pl.loop(0, peers)
     def _(index):
@@ -433,19 +507,19 @@
 def renew(grad, sums, loss, field, probe, last):
     devices = lax.axis_size("row")
     peers = devices // 2
-    planes, parts, extent, width = field.shape
+    planes, parts, tiles, extent, _ = field.shape
     piece = sums.shape[1] // devices
     reach = MARGIN if last else 2 * MARGIN
-    height = extent - 2 * MARGIN if last else extent
+    shape = (planes, parts, extent - 2 * MARGIN, tiles * LANES) if last else field.shape
     vmem = pl.BlockSpec(memory_space=pltpu.VMEM)
-    edge = pltpu.VMEM((planes, parts, reach, width), jnp.float32)
+    edge = pltpu.VMEM((planes, parts, tiles, reach, LANES), jnp.float32)
     packet = pltpu.VMEM((peers, 3 * piece + 8, LANES), jnp.float32)
     each = pltpu.SemaphoreType.DMA((peers,))
     two = pltpu.SemaphoreType.DMA((2,))
     return pl.pallas_call(
         functools.partial(renew_kernel, devices, last),
         out_shape=(
-            jax.ShapeDtypeStruct((planes, parts, height, width), jnp.float32),
+            jax.ShapeDtypeStruct(shape, jnp.float32),
             jax.ShapeDtypeStruct(probe.shape, jnp.float32),
             jax.ShapeDtypeStruct(loss.shape, jnp.float32),
         ),

time: 134 us -> 123 us (0.918)
  the two profiles are of different devices: /device:TPU:1 before, /device:TPU:9 now
where the time goes in v3:
time: 123 us
  Pallas kernels  103 us (84%)
  local copies, waits for them, and re-layouts  15.5 us (13%)
  between operations  2.05 us (2%)
  other arithmetic  1.78 us (1%)
    pallas_call x2, Pallas kernels, renew(): pl.pallas_call(functools.partial(renew_kernel, devices, last), out_shape=...  66.3 us
    pallas_call x2, Pallas kernels, local_terms(): pl.pallas_call(local_kernel, out_shape=(jax.ShapeDtypeStruct(field.shape,...  25.5 us
    unnamed x31, local copies, waits for them, and re-layouts  13.6 us
    pallas_call x1, Pallas kernels, first_field(): pl.pallas_call(functools.partial(first_kernel, lax.axis_size('row')), out...  11.5 us

profile of v3, /device:TPU:9, one launch (start us, length us, event | category | flops | bytes accessed | tf_op | source)
XLA Modules:
  0.0 122.7 jit_solution(13923312388639281992)
XLA Ops:
  0.6 0.0 copy-start
  0.6 1.0 copy-done
  1.7 0.0 copy-start.6
  1.7 0.0 copy-start.12
  1.7 0.0 copy-start.13
  1.7 0.0 copy-start.14
  1.7 0.0 copy-start.9
  1.7 1.3 %copy-done.9 = f32[2,2,192,384]{3,2,1,0:T(8,128)S(1)} copy-done((f32[2,2,192,384]{3,2,1,0:T(8,128)S(1)}, f32[2,2,192,384]{3,2,1,0:T(8,128)}, u32[]{:S(2)}) %copy-start.9) | copy-done | bytes 1179672
  3.1 0.0 copy-start.3
  3.1 0.0 copy-start.4
  3.1 11.5 %shard_map.121.field = f32[2,2,3,320,128]{4,3,2,1,0:T(8,128)S(1)} custom-call(f32[2,2,192,384]{3,2,1,0:T(8,128)S(1)} %copy-done.9), custom_call_target="tpu_custom_call" | custom-call | tf_op jit(solution)/shard_map/pallas_call | solution.py:283
  14.6 0.0 copy-start.1
  14.6 1.3 %copy-done.1 = f32[2,2,3,320,128]{4,3,2,1,0:T(8,128)} copy-done((f32[2,2,3,320,128]{4,3,2,1,0:T(8,128)}, f32[2,2,3,320,128]{4,3,2,1,0:T(8,128)S(1)}, u32[]{:S(2)}) %copy-start.1) | copy-done | bytes 1966104
  15.9 0.0 copy-done.6
  15.9 0.0 copy-done.12
  15.9 0.0 copy-done.13
  15.9 0.0 copy-done.14
  15.9 0.0 copy-done.3
  15.9 0.0 copy-done.4
  15.9 12.7 %shard_map.122 = (f32[2,2,3,320,128]{4,3,2,1,0:T(8,128)}, f32[3,512,128]{2,1,0:T(8,128)S(1)}, f32[8,128]{1,0:T(8,128)S(1)}) custom-call(s32[2]{0:T(128)S(1)} %copy-done.12, s32[2]{0:T(128)S(1)} %copy-done.13, s32[2]{0:T(128)S(1)} %copy-done.14, f32[2,2,3,320,128]{4,3,2,1,0:T(8,128)} %copy-done.1, f32[2,512,128]{2,1,0:T(8,128)S(1)} %bitcast.17, ...), custom_call_target="tpu_custom_call" | custom-call | tf_op jit(solution)/shard_map/pallas_call | solution.py:191
  28.7 0.0 copy-start.8
  28.7 1.5 %copy-done.8 = f32[2,2,3,320,128]{4,3,2,1,0:T(8,128)S(1)} copy-done((f32[2,2,3,320,128]{4,3,2,1,0:T(8,128)S(1)}, f32[2,2,3,320,128]{4,3,2,1,0:T(8,128)}, u32[]{:S(2)}) %copy-start.8) | copy-done | bytes 1966104
  30.2 38.5 %shard_map.123 = (f32[2,2,3,320,128]{4,3,2,1,0:T(8,128)S(1)}, f32[2,512,128]{2,1,0:T(8,128)S(1)}, f32[8,128]{1,0:T(8,128)S(1)}) custom-call(f32[2,2,3,320,128]{4,3,2,1,0:T(8,128)S(1)} %copy-done.8, f32[3,512,128]{2,1,0:T(8,128)S(1)} %get-tuple-element.16.sums, f32[8,128]{1,0:T(8,128)S(1)} %get-tuple-element.17.loss, f32[2,2,3,320,128]{4,3,2,1,0:T(8,128)} %copy-done.1, ...), custom_call_target="tpu_custom_call" | custom-call | tf_op jit(solution)/shard_map/pallas_call | solution.py:519
  68.8 0.0 copy-start.2
  68.8 1.3 %copy-done.2 = f32[2,2,3,320,128]{4,3,2,1,0:T(8,128)} copy-done((f32[2,2,3,320,128]{4,3,2,1,0:T(8,128)}, f32[2,2,3,320,128]{4,3,2,1,0:T(8,128)S(1)}, u32[]{:S(2)}) %copy-start.2) | copy-done | bytes 1966104
  70.1 0.6 reduce_sum.18
  71.3 0.0 copy-start.5
  71.3 1.4 %copy-done.5 = bf16[512,1536]{1,0:T(8,128)(2,1)S(1)} copy-done((bf16[512,1536]{1,0:T(8,128)(2,1)S(1)}, bf16[512,1536]{1,0:T(8,128)(2,1)}, u32[]{:S(2)}) %copy-start.5) | copy-done | bytes 1572888
  72.7 12.8 %shard_map.124 = (f32[2,2,3,320,128]{4,3,2,1,0:T(8,128)}, f32[3,512,128]{2,1,0:T(8,128)S(1)}, f32[8,128]{1,0:T(8,128)S(1)}) custom-call(s32[2]{0:T(128)S(1)} %copy-done.12, s32[2]{0:T(128)S(1)} %copy-done.13, s32[2]{0:T(128)S(1)} %copy-done.14, f32[2,2,3,320,128]{4,3,2,1,0:T(8,128)} %copy-done.2, f32[2,512,128]{2,1,0:T(8,128)S(1)} %get-tuple-element.19.probe, ...), custom_call_target="tpu_custom_call" | custom-call | tf_op jit(solution)/shard_map/pallas_call | solution.py:191
  85.5 0.0 copy-start.7
  85.5 1.5 %copy-done.7 = f32[2,2,3,320,128]{4,3,2,1,0:T(8,128)S(1)} copy-done((f32[2,2,3,320,128]{4,3,2,1,0:T(8,128)S(1)}, f32[2,2,3,320,128]{4,3,2,1,0:T(8,128)}, u32[]{:S(2)}) %copy-start.7) | copy-done | bytes 1966104
  87.0 27.7 %shard_map.125 = (f32[2,2,192,384]{3,2,1,0:T(8,128)S(1)}, f32[2,512,128]{2,1,0:T(8,128)S(1)}, f32[8,128]{1,0:T(8,128)S(1)}) custom-call(f32[2,2,3,320,128]{4,3,2,1,0:T(8,128)S(1)} %copy-done.7, f32[3,512,128]{2,1,0:T(8,128)S(1)} %get-tuple-element.21.sums, f32[8,128]{1,0:T(8,128)S(1)} %get-tuple-element.22.loss, f32[2,2,3,320,128]{4,3,2,1,0:T(8,128)} %copy-done.2, ...), custom_call_target="tpu_custom_call" | custom-call | tf_op jit(solution)/shard_map/pallas_call | solution.py:519
  114.8 0.0 copy-start.10
  114.8 1.0 copy-done.10
  115.8 0.0 copy-start.11
  115.8 0.8 copy-done.11
  116.6 0.6 reduce_sum.19
  117.8 0.6 pad_maximum_fusion
  118.4 1.9 %copy.19 = f32[2,2,32,8,128]{4,3,1,2,0:T(8,128)} copy(f32[2,2,32,8,128]{4,3,2,1,0:T(8,128)} %bitcast.19) | data formatting | bytes 1048576 | tf_op jit(solution)/shard_map/reshape | solution.py:559
  120.3 2.4 %copy.21 = f32[2,2,192,384]{3,2,1,0:T(8,128)} copy(f32[2,2,192,384]{3,2,1,0:T(8,128)} %copy-done.10) | data formatting | bytes 2359296
  (1 shorter events, 0.0 us)
Async XLA Ops:
  0.6 1.0 copy-start
  1.7 14.2 %copy-start.6 = (f32[2,256,256]{2,1,0:T(8,128)S(1)}, f32[2,256,256]{2,1,0:T(8,128)}, u32[]{:S(2)}) copy-start(f32[2,256,256]{2,1,0:T(8,128)} %intensity.3) | copy-start | bytes 1572868
  1.7 14.2 %copy-start.12 = (s32[2]{0:T(128)S(1)}, s32[2]{0:T(128)}, u32[]{:S(2)}) copy-start(s32[2]{0:T(128)} %rows_ref.3) | copy-start | bytes 28
  1.7 14.2 %copy-start.13 = (s32[2]{0:T(128)S(1)}, s32[2]{0:T(128)}, u32[]{:S(2)}) copy-start(s32[2]{0:T(128)} %cols_ref.3) | copy-start | bytes 28
  1.7 14.2 %copy-start.14 = (s32[2]{0:T(128)S(1)}, s32[2]{0:T(128)}, u32[]{:S(2)}) copy-start(s32[2]{0:T(128)} %first_ref.3) | copy-start | bytes 28
  1.7 1.3 %copy-start.9 = (f32[2,2,192,384]{3,2,1,0:T(8,128)S(1)}, f32[2,2,192,384]{3,2,1,0:T(8,128)}, u32[]{:S(2)}) copy-start(f32[2,2,192,384]{3,2,1,0:T(8,128)} %own.1) | copy-start | bytes 3538948
  3.1 12.9 %copy-start.3 = (bf16[1536,512]{1,0:T(8,128)(2,1)S(1)}, bf16[1536,512]{1,0:T(8,128)(2,1)}, u32[]{:S(2)}) copy-start(bf16[1536,512]{1,0:T(8,128)(2,1)} %constant.15.clone.dft_r) | copy-start | bytes 4718596
  3.1 12.9 %copy-start.4 = (bf16[512,1536]{1,0:T(8,128)(2,1)S(1)}, bf16[512,1536]{1,0:T(8,128)(2,1)}, u32[]{:S(2)}) copy-start(bf16[512,1536]{1,0:T(8,128)(2,1)} %constant.14.clone.dft_l) | copy-start | bytes 4718596
  14.6 1.3 %copy-start.1 = (f32[2,2,3,320,128]{4,3,2,1,0:T(8,128)}, f32[2,2,3,320,128]{4,3,2,1,0:T(8,128)S(1)}, u32[]{:S(2)}) copy-start(f32[2,2,3,320,128]{4,3,2,1,0:T(8,128)S(1)} %shard_map.121.field) | copy-start | bytes 5898244
  28.7 1.5 %copy-start.8 = (f32[2,2,3,320,128]{4,3,2,1,0:T(8,128)S(1)}, f32[2,2,3,320,128]{4,3,2,1,0:T(8,128)}, u32[]{:S(2)}) copy-start(f32[2,2,3,320,128]{4,3,2,1,0:T(8,128)} %get-tuple-element.15.grad) | copy-start | bytes 5898244
  68.8 1.3 %copy-start.2 = (f32[2,2,3,320,128]{4,3,2,1,0:T(8,128)}, f32[2,2,3,320,128]{4,3,2,1,0:T(8,128)S(1)}, u32[]{:S(2)}) copy-start(f32[2,2,3,320,128]{4,3,2,1,0:T(8,128)S(1)} %get-tuple-element.18.field) | copy-start | bytes 5898244
  71.3 1.4 %copy-start.5 = (bf16[512,1536]{1,0:T(8,128)(2,1)S(1)}, bf16[512,1536]{1,0:T(8,128)(2,1)}, u32[]{:S(2)}) copy-start(bf16[512,1536]{1,0:T(8,128)(2,1)} %constant.14.clone.dft_l) | copy-start | bytes 4718596
  85.5 1.5 %copy-start.7 = (f32[2,2,3,320,128]{4,3,2,1,0:T(8,128)S(1)}, f32[2,2,3,320,128]{4,3,2,1,0:T(8,128)}, u32[]{:S(2)}) copy-start(f32[2,2,3,320,128]{4,3,2,1,0:T(8,128)} %get-tuple-element.20.grad) | copy-start | bytes 5898244
  114.8 1.0 copy-start.10
  115.8 0.8 copy-start.11

commit v4 on v3

--- a/solution.py
+++ b/solution.py
@@ -231,7 +231,9 @@
     )
 
 
-def first_kernel(devices, own, field, above, below, send_sem, recv_sem):
+def first_kernel(
+    devices, own, probe, field, light, above, below, send_sem, recv_sem
+):
     me = lax.axis_index("row")
     tile = own.shape[2]
     has_before, has_after = me > 0, me < devices - 1
@@ -253,6 +255,10 @@
             )
 
     place(MARGIN, tile, own)
+    length = probe.shape[1]
+    for part in range(length // LANES):
+        columns = slice(part * LANES, (part + 1) * LANES)
+        light[:, part * length : (part + 1) * length] = probe[:, :, columns]
 
     @pl.when(has_before)
     def _():
@@ -276,61 +282,93 @@
     pl.when(has_after)(down.wait_send)
 
 
-def first_field(own):
+def first_field(own, probe):
     planes, parts, tile, width = own.shape
     vmem = pl.BlockSpec(memory_space=pltpu.VMEM)
     edge = pltpu.VMEM((planes, parts, MARGIN, width), jnp.float32)
     return pl.pallas_call(
         functools.partial(first_kernel, lax.axis_size("row")),
-        out_shape=jax.ShapeDtypeStruct(
-            (planes, parts, width // LANES, tile + 2 * MARGIN, LANES), jnp.float32
+        out_shape=(
+            jax.ShapeDtypeStruct(
+                (planes, parts, width // LANES, tile + 2 * MARGIN, LANES), jnp.float32
+            ),
+            jax.ShapeDtypeStruct((2, probe[0].size // LANES, LANES), jnp.float32),
         ),
-        in_specs=[vmem],
-        out_specs=vmem,
+        in_specs=[vmem] * 2,
+        out_specs=(vmem,) * 2,
         scratch_shapes=[edge, edge, pltpu.SemaphoreType.DMA((2,)), pltpu.SemaphoreType.DMA((2,))],
         compiler_params=pltpu.CompilerParams(
             collective_id=0, has_side_effects=True, vmem_limit_bytes=VMEM_LIMIT
         ),
-    )(own)
-
-
-def renew_kernel(
-    devices, last, grad, sums, loss, field, probe, field_out, probe_out, loss_out,
-    from_pair, loss_pair, to_peer, from_peer, renewed, above, below,
-    pair_send, pair_recv, loss_sem, peer_send, peer_recv, spread_send, spread_recv,
-    back_send, back_recv, edge_send, edge_recv,
-):
+    )(own, probe)
+
+
+def object_rate(probe):
+    square = probe[0] * probe[0] + probe[1] * probe[1]
+    return OBJECT_RATE / (jnp.sum(square, keepdims=True) / square.size + TINY)
+
+
+def planes_of(ref):
+    first, second, third = ref.shape[:3]
+    return [(i, j, k) for i in range(first) for j in range(second) for k in range(third)]
+
+
+def renew_kernel(devices, last, grad, sums, loss, probe, *refs):
+    if last:
+        above_out, below_out, probe_out, loss_out, *refs = refs
+    else:
+        field, field_out, probe_out, loss_out, *refs = refs
+    (
+        from_pair, loss_of, to_mate, from_mate, to_peer, from_peer, renewed, above, below,
+        loss_send, loss_recv, pair_send, pair_recv, mate_send, mate_recv, peer_send, peer_recv,
+        spread_send, spread_recv, cross_send, cross_recv, back_send, back_recv,
+        edge_send, edge_recv,
+    ) = refs
     me = lax.axis_index("row")
-    peers = devices // 2
-    core, place = lax.rem(me, 2), lax.div(me, 2)
-    partner = me + 1 - 2 * core
+    peers = devices // 4
+    core, side, place = lax.rem(me, 2), lax.rem(lax.div(me, 2), 2), lax.div(me, 4)
+    partner, mate = me + 1 - 2 * core, me + 2 - 4 * side
     piece = sums.shape[1] // devices
-    extent = field.shape[3]
+    extent = grad.shape[3]
     reach = above.shape[3]
     has_before, has_after = me > 0, me < devices - 1
 
-    def rows_of(side, index):
-        return pl.ds(pl.multiple_of((side * peers + index) * piece, piece), piece)
-
-    def to_pair(index, side):
+    def rows_of(core_at, side_at, index):
+        start = ((core_at * 2 + side_at) * peers + index) * piece
+        return pl.ds(pl.multiple_of(start, piece), piece)
+
+    def to_pair(side_at, index, core_at):
         return send(
-            sums.at[:, rows_of(side, index)], from_pair.at[index],
-            pair_send.at[index], pair_recv.at[index], partner,
+            sums.at[:, rows_of(core_at, side_at, index)], from_pair.at[side_at, index],
+            pair_send.at[side_at, index], pair_recv.at[side_at, index], partner,
+        )
+
+    def to_side(index):
+        return send(
+            to_mate.at[index], from_mate.at[index], mate_send.at[index], mate_recv.at[index], mate
         )
 
     def to_place(index, slot):
         return send(
             to_peer.at[index], from_peer.at[slot],
-            peer_send.at[index], peer_recv.at[slot], 2 * index + core,
+            peer_send.at[index], peer_recv.at[slot], 4 * index + 2 * side + core,
         )
 
     def spread(index, slot):
-        part = renewed.at[:, rows_of(core, slot)]
-        return send(part, part, spread_send.at[index], spread_recv.at[slot], 2 * index + core)
-
-    def back(index, side):
-        part = renewed.at[:, rows_of(side, index)]
-        return send(part, part, back_send.at[index], back_recv.at[index], partner)
+        part = renewed.at[:, rows_of(core, side, slot)]
+        return send(
+            part, part, spread_send.at[index], spread_recv.at[slot], 4 * index + 2 * side + core
+        )
+
+    def cross(side_at, index):
+        part = renewed.at[:, rows_of(core, side_at, index)]
+        return send(part, part, cross_send.at[index], cross_recv.at[index], mate)
+
+    def back(core_at, side_at, index):
+        part = renewed.at[:, rows_of(core_at, side_at, index)]
+        return send(
+            part, part, back_send.at[side_at, index], back_recv.at[side_at, index], partner
+        )
 
     def after_me(step):
         return lax.rem(place + 1 + step, peers)
@@ -339,63 +377,82 @@
         return lax.rem(place + peers - 1 - step, peers)
 
     other = me - 1 + 2 * core
+    beside = (other >= 0) & (other < devices)
     barrier = pltpu.get_barrier_semaphore()
 
     def signal(device):
         pl.semaphore_signal(barrier, inc=1, device_id={"row": device}, device_id_type=MESH)
 
     signal(partner)
+    signal(mate)
 
     @pl.loop(0, peers - 1)
     def _(step):
-        signal(2 * after_me(step) + core)
-
-    beside = (other >= 0) & (other < devices)
+        signal(4 * after_me(step) + 2 * side + core)
 
     @pl.when(beside)
     def _():
         signal(other)
 
-    pl.semaphore_wait(barrier, peers + beside.astype(jnp.int32))
-
-    to_loss = send(loss, loss_pair, loss_sem.at[0], loss_sem.at[1], partner)
-    to_loss.start()
+    pl.semaphore_wait(barrier, peers + 1 + beside.astype(jnp.int32))
+
+    pair_loss = send(loss, loss_of.at[0], loss_send.at[0], loss_recv.at[0], partner)
+    mate_loss = send(loss_of.at[1], loss_of.at[2], loss_send.at[1], loss_recv.at[1], mate)
+    pair_loss.start()
 
     @pl.loop(0, peers)
     def _(step):
-        to_pair(after_me(step), 1 - core).start()
-
-    up = send(grad.at[:, :, :, pl.ds(0, reach)], below, edge_send.at[0], edge_recv.at[0], me - 1)
+        to_pair(1 - side, after_me(step), 1 - core).start()
+
+    @pl.loop(0, peers)
+    def _(step):
+        to_pair(side, after_me(step), 1 - core).start()
+
+    up = send(
+        grad.at[:, :, :, pl.ds(0, reach)], below, edge_send.at[0], edge_recv.at[0], me - 1
+    )
     down = send(
-        grad.at[:, :, :, pl.ds(extent - reach, reach)], above, edge_send.at[1], edge_recv.at[1], me + 1
-    )
-    pl.when(core == 1)(up.start)
-    pl.when(core == 0)(down.start)
-
-    to_loss.wait()
-    pair_loss = loss[...] + loss_pair[...]
-
-    def add_pair(index):
-        to_pair(index, core).wait_recv()
-        both = sums[:, rows_of(core, index), :] + from_pair[index]
-        return both
+        grad.at[:, :, :, pl.ds(extent - reach, reach)], above,
+        edge_send.at[1], edge_recv.at[1], me + 1,
+    )
+
+    pair_loss.wait()
+    loss_of[1] = loss[...] + loss_of[0]
+    mate_loss.start()
+
+    def add_pair(side_at, index):
+        to_pair(side_at, index, core).wait_recv()
+        return sums[:, rows_of(core, side_at, index), :] + from_pair[side_at, index]
+
+    @pl.loop(0, peers)
+    def _(step):
+        index = after_me(step)
+        to_mate[index] = add_pair(1 - side, index)
+        to_side(index).start()
+
+    pl.when(has_before)(up.start)
+    pl.when(has_after)(down.start)
+
+    mate_loss.wait()
+    quad_loss = loss_of[1] + loss_of[2]
+
+    def fill(target, slot, index):
+        both = add_pair(side, index)
+        to_side(index).wait_recv()
+        both = both + from_mate[index]
+        for plane in range(3):
+            target[slot, plane * piece : (plane + 1) * piece] = both[plane]
+        target[slot, 3 * piece :] = quad_loss
 
     @pl.loop(0, peers - 1)
     def _(step):
         index = after_me(step)
-        both = add_pair(index)
-        for plane in range(3):
-            to_peer[index, plane * piece : (plane + 1) * piece] = both[plane]
-        to_peer[index, 3 * piece :] = pair_loss
+        fill(to_peer, index, index)
         to_place(index, place).start()
 
-    both = add_pair(place)
-    for plane in range(3):
-        from_peer[place, plane * piece : (plane + 1) * piece] = both[plane]
-    from_peer[place, 3 * piece :] = pair_loss
-
-    square = probe[0] * probe[0] + probe[1] * probe[1]
-    rate = OBJECT_RATE / (jnp.sum(square, keepdims=True) / (square.size) + TINY)
+    fill(from_peer, place, place)
+
+    rate = object_rate(probe)
 
     @pl.loop(0, peers - 1)
     def _(step):
@@ -406,7 +463,7 @@
     for index in range(1, peers):
         total = total + from_peer[index]
     loss_out[...] = total[3 * piece :]
-    mine = rows_of(core, place)
+    mine = rows_of(core, side, place)
     weight = total[2 * piece : 3 * piece] + DAMPING
     for part in range(2):
         step = PROBE_RATE * total[part * piece : (part + 1) * piece] / weight
@@ -416,36 +473,26 @@
     def _(step):
         spread(after_me(step), place).start()
 
-    back(place, core).start()
-    pl.when((core == 0) & has_before)(up.start)
-    pl.when((core == 1) & has_after)(down.start)
-
-    first_row = MARGIN if last else 0
-    planes = [
-        (which, part, index)
-        for which in range(grad.shape[0])
-        for part in range(grad.shape[1])
-        for index in range(grad.shape[2])
-    ]
-
-    def put(plane, start, value):
-        rows = slice(start, start + value.shape[0])
-        if last:
-            which, part, index = plane
-            field_out[which, part, rows, index * LANES : (index + 1) * LANES] = value
-        else:
-            field_out[(*plane, rows)] = value
-
-    low, high = reach + first_row, extent - reach - first_row
-    for plane in planes:
-        rows = (*plane, slice(low, high))
-        put(plane, reach, field[rows] - rate * grad[rows])
+    cross(side, place).start()
+    back(core, side, place).start()
+
+    if not last:
+        for plane in planes_of(grad):
+            rows = (*plane, slice(reach, extent - reach))
+            field_out[rows] = field[rows] - rate * grad[rows]
 
     @pl.loop(0, peers - 1)
     def _(step):
         index = before_me(step)
         spread(index, index).wait_recv()
-        back(index, core).start()
+        cross(side, index).start()
+        back(core, side, index).start()
+
+    @pl.loop(0, peers)
+    def _(step):
+        index = lax.rem(place + peers - step, peers)
+        cross(1 - side, index).wait_recv()
+        back(core, 1 - side, index).start()
 
     @pl.when(has_before)
     def _():
@@ -455,9 +502,12 @@
     def _():
         above[...] = jnp.zeros_like(above)
 
-    for plane in planes:
-        rows = (*plane, slice(first_row, first_row + reach))
-        put(plane, 0, field[rows] - rate * (grad[rows] + above[plane]))
+    if last:
+        above_out[...] = above[...]
+    else:
+        for plane in planes_of(grad):
+            rows = (*plane, slice(0, reach))
+            field_out[rows] = field[rows] - rate * (grad[rows] + above[plane])
 
     @pl.when(has_after)
     def _():
@@ -467,32 +517,41 @@
     def _():
         below[...] = jnp.zeros_like(below)
 
-    for plane in planes:
-        rows = (*plane, slice(extent - first_row - reach, extent - first_row))
-        put(plane, extent - 2 * first_row - reach, field[rows] - rate * (grad[rows] + below[plane]))
-
-    if not last:
+    if last:
+        below_out[...] = below[...]
+    else:
+        for plane in planes_of(grad):
+            rows = (*plane, slice(extent - reach, extent))
+            field_out[rows] = field[rows] - rate * (grad[rows] + below[plane])
+        empty = (*field.shape[:3], MARGIN, LANES)
 
         @pl.when(me == 0)
         def _():
-            field_out[:, :, :, :MARGIN] = jnp.zeros((*field.shape[:3], MARGIN, LANES), jnp.float32)
+            field_out[:, :, :, :MARGIN] = jnp.zeros(empty, jnp.float32)
 
         @pl.when(me == devices - 1)
         def _():
-            field_out[:, :, :, extent - MARGIN :] = jnp.zeros(
-                (*field.shape[:3], MARGIN, LANES), jnp.float32
-            )
+            field_out[:, :, :, extent - MARGIN :] = jnp.zeros(empty, jnp.float32)
+
+    for side_at in range(2):
+
+        @pl.loop(0, peers)
+        def _(index, side_at=side_at):
+            back(1 - core, side_at, index).wait_recv()
+
+    probe_out[...] = renewed[...]
+
+    for side_at in range(2):
+
+        @pl.loop(0, peers)
+        def _(index, side_at=side_at):
+            to_pair(side_at, index, 1 - core).wait_send()
+            back(core, side_at, index).wait_send()
 
     @pl.loop(0, peers)
     def _(index):
-        back(index, 1 - core).wait_recv()
-
-    probe_out[...] = renewed[...]
-
-    @pl.loop(0, peers)
-    def _(index):
-        to_pair(index, 1 - core).wait_send()
-        back(index, core).wait_send()
+        to_side(index).wait_send()
+        cross(side, index).wait_send()
 
     @pl.loop(0, peers - 1)
     def _(step):
@@ -506,57 +565,102 @@
 
 def renew(grad, sums, loss, field, probe, last):
     devices = lax.axis_size("row")
-    peers = devices // 2
-    planes, parts, tiles, extent, _ = field.shape
+    peers = devices // 4
     piece = sums.shape[1] // devices
     reach = MARGIN if last else 2 * MARGIN
-    shape = (planes, parts, extent - 2 * MARGIN, tiles * LANES) if last else field.shape
     vmem = pl.BlockSpec(memory_space=pltpu.VMEM)
-    edge = pltpu.VMEM((planes, parts, tiles, reach, LANES), jnp.float32)
+    edge_shape = (*field.shape[:3], reach, LANES)
+    edge = pltpu.VMEM(edge_shape, jnp.float32)
+    edge_out = jax.ShapeDtypeStruct(edge_shape, jnp.float32)
     packet = pltpu.VMEM((peers, 3 * piece + 8, LANES), jnp.float32)
+    part = pltpu.VMEM((peers, 3, piece, LANES), jnp.float32)
     each = pltpu.SemaphoreType.DMA((peers,))
+    double = pltpu.SemaphoreType.DMA((2, peers))
     two = pltpu.SemaphoreType.DMA((2,))
+    objects = (edge_out, edge_out) if last else (jax.ShapeDtypeStruct(field.shape, jnp.float32),)
+    outs = objects + (
+        jax.ShapeDtypeStruct(probe.shape, jnp.float32),
+        jax.ShapeDtypeStruct(loss.shape, jnp.float32),
+    )
+    operands = (grad, sums, loss, probe) + (() if last else (field,))
     return pl.pallas_call(
         functools.partial(renew_kernel, devices, last),
-        out_shape=(
-            jax.ShapeDtypeStruct(shape, jnp.float32),
-            jax.ShapeDtypeStruct(probe.shape, jnp.float32),
-            jax.ShapeDtypeStruct(loss.shape, jnp.float32),
-        ),
-        in_specs=[vmem] * 5,
-        out_specs=(vmem,) * 3,
+        out_shape=outs,
+        in_specs=[vmem] * len(operands),
+        out_specs=(vmem,) * len(outs),
         scratch_shapes=[
-            pltpu.VMEM((peers, 3, piece, LANES), jnp.float32),
-            pltpu.VMEM(loss.shape, jnp.float32),
+            pltpu.VMEM((2, peers, 3, piece, LANES), jnp.float32),
+            pltpu.VMEM((3, *loss.shape), jnp.float32),
+            part,
+            part,
             packet,
             packet,
             pltpu.VMEM(probe.shape, jnp.float32),
             edge,
             edge,
-            each, each, two, each, each, each, each, each, each, two, two,
+            two, two, double, double, each, each, each, each,
+            each, each, each, each, double, double,
+            two, two,
         ],
         compiler_params=pltpu.CompilerParams(
             collective_id=2 if last else 1, has_side_effects=True, vmem_limit_bytes=VMEM_LIMIT
         ),
-    )(grad, sums, loss, field, probe)
+    )(*operands)
+
+
+def finish_kernel(
+    count, field, grad, above, below, old, probe, *refs
+):
+    *losses, field_out, probe_out, misfit_out = refs
+    rate = object_rate(old)
+    length = probe_out.shape[1]
+    tile = field_out.shape[2]
+    for plane in planes_of(field):
+        which, part, index = plane
+        columns = slice(index * LANES, (index + 1) * LANES)
+        for start, stop, extra in (
+            (0, MARGIN, above), (MARGIN, tile - MARGIN, None), (tile - MARGIN, tile, below)
+        ):
+            rows = (*plane, slice(MARGIN + start, MARGIN + stop))
+            value = grad[rows] if extra is None else grad[rows] + extra[plane]
+            field_out[which, part, start:stop, columns] = field[rows] - rate * value
+    for part in range(length // LANES):
+        columns = slice(part * LANES, (part + 1) * LANES)
+        probe_out[:, :, columns] = probe[:, part * length : (part + 1) * length]
+    for index, loss in enumerate(losses):
+        misfit_out[index] = jnp.sum(loss[...]) / count
+
+
+def finish(count, field, grad, above, below, old, probe, losses, shapes):
+    vmem = pl.BlockSpec(memory_space=pltpu.VMEM)
+    return pl.pallas_call(
+        functools.partial(finish_kernel, count),
+        out_shape=tuple(
+            jax.ShapeDtypeStruct(shape, jnp.float32) for shape in (*shapes, (len(losses),))
+        ),
+        in_specs=[vmem] * (6 + len(losses)),
+        out_specs=(vmem, vmem, pl.BlockSpec(memory_space=pltpu.SMEM)),
+        compiler_params=pltpu.CompilerParams(vmem_limit_bytes=VMEM_LIMIT),
+    )(field, grad, above, below, old, probe, *losses)
 
 
 def shards(object_field, probe, intensity, row_offset, col_offset, slice_first):
     length = probe.shape[1]
-    parts = length // LANES
-    count = intensity.shape[0] * lax.axis_size("row") * length * length
-    light = probe.reshape(2, length, parts, LANES).transpose(0, 2, 1, 3)
-    light = light.reshape(2, parts * length, LANES)
-    field = first_field(object_field)
+    count = float(intensity.shape[0] * lax.axis_size("row") * length * length)
+    field, light = first_field(object_field, probe)
     losses = []
     for step in range(ITERS):
         grad, sums, loss = local_terms(
             field, light, intensity, row_offset, col_offset, slice_first
         )
-        field, light, loss = renew(grad, sums, loss, field, light, step == ITERS - 1)
-        losses.append(jnp.sum(loss) / count)
-    light = light.reshape(2, parts, length, LANES).transpose(0, 2, 1, 3)
-    return field, light.reshape(probe.shape), jnp.stack(losses)
+        old = light
+        if step < ITERS - 1:
+            field, light, loss = renew(grad, sums, loss, field, light, False)
+        else:
+            above, below, light, loss = renew(grad, sums, loss, field, light, True)
+        losses.append(loss)
+    shapes = (object_field.shape, probe.shape)
+    return finish(count, field, grad, above, below, old, light, losses, shapes)
 
 
 def solution(mesh):

time: 123 us -> 112 us (0.911)
  the two profiles are of different devices: /device:TPU:9 before, /device:TPU:1 now
where the time goes in v4:
time: 112 us
  Pallas kernels  98.9 us (88%)
  local copies, waits for them, and re-layouts  12.1 us (11%)
    pallas_call x2, Pallas kernels, renew(): pl.pallas_call(functools.partial(renew_kernel, devices, last), out_shape=...  60.3 us
    pallas_call x2, Pallas kernels, local_terms(): pl.pallas_call(local_kernel, out_shape=(jax.ShapeDtypeStruct(field.shape,...  25.4 us
    unnamed x32, local copies, waits for them, and re-layouts  12.1 us
    pallas_call x1, Pallas kernels, first_field(): pl.pallas_call(functools.partial(first_kernel, lax.axis_size('row')), out...  11.6 us

profile of v4, /device:TPU:1, one launch (start us, length us, event | category | flops | bytes accessed | tf_op | source)
XLA Modules:
  0.0 111.8 jit_solution(2258359477085170236)
XLA Ops:
  0.6 0.0 copy-start.5
  0.6 0.0 copy-start.11
  0.7 1.4 %copy-done.11 = f32[2,2,192,384]{3,2,1,0:T(8,128)S(1)} copy-done((f32[2,2,192,384]{3,2,1,0:T(8,128)S(1)}, f32[2,2,192,384]{3,2,1,0:T(8,128)}, u32[]{:S(2)}) %copy-start.11) | copy-done | bytes 1179672
  2.0 0.0 copy-start.12
  2.0 1.0 copy-done.12
  3.1 0.0 copy-start.13
  3.1 0.0 copy-start.14
  3.1 0.0 copy-start.15
  3.1 11.6 %shard_map.121 = (f32[2,2,3,320,128]{4,3,2,1,0:T(8,128)S(1)}, f32[2,512,128]{2,1,0:T(8,128)S(1)}) custom-call(f32[2,2,192,384]{3,2,1,0:T(8,128)S(1)} %copy-done.11, f32[2,256,256]{2,1,0:T(8,128)S(1)} %copy-done.12), custom_call_target="tpu_custom_call" | custom-call | tf_op jit(solution)/shard_map/pallas_call | solution.py:289
  14.7 0.0 copy-start.2
  14.7 1.3 %copy-done.2 = f32[2,2,3,320,128]{4,3,2,1,0:T(8,128)} copy-done((f32[2,2,3,320,128]{4,3,2,1,0:T(8,128)}, f32[2,2,3,320,128]{4,3,2,1,0:T(8,128)S(1)}, u32[]{:S(2)}) %copy-start.2) | copy-done | bytes 1966104
  16.0 0.0 copy-done.5
  16.0 0.0 copy-done.13
  16.0 0.0 copy-done.14
  16.0 0.0 copy-done.15
  16.0 0.0 copy-start.6
  16.0 1.4 %copy-done.6 = bf16[512,1536]{1,0:T(8,128)(2,1)S(1)} copy-done((bf16[512,1536]{1,0:T(8,128)(2,1)S(1)}, bf16[512,1536]{1,0:T(8,128)(2,1)}, u32[]{:S(2)}) %copy-start.6) | copy-done | bytes 1572888
  17.4 0.0 copy-start.8
  17.4 1.0 copy-done.8
  18.5 12.7 %shard_map.122 = (f32[2,2,3,320,128]{4,3,2,1,0:T(8,128)}, f32[3,512,128]{2,1,0:T(8,128)S(1)}, f32[8,128]{1,0:T(8,128)S(1)}) custom-call(s32[2]{0:T(128)S(1)} %copy-done.13, s32[2]{0:T(128)S(1)} %copy-done.14, s32[2]{0:T(128)S(1)} %copy-done.15, f32[2,2,3,320,128]{4,3,2,1,0:T(8,128)} %copy-done.2, f32[2,512,128]{2,1,0:T(8,128)S(1)} %get-tuple-element.19.probe, ...), custom_call_target="tpu_custom_call" | custom-call | tf_op jit(solution)/shard_map/pallas_call | solution.py:191
  31.1 0.0 copy-start.10
  31.2 1.5 %copy-done.10 = f32[2,2,3,320,128]{4,3,2,1,0:T(8,128)S(1)} copy-done((f32[2,2,3,320,128]{4,3,2,1,0:T(8,128)S(1)}, f32[2,2,3,320,128]{4,3,2,1,0:T(8,128)}, u32[]{:S(2)}) %copy-start.10) | copy-done | bytes 1966104
  32.7 0.0 copy-start.7
  32.7 0.0 copy-start.9
  32.7 34.3 %shard_map.123 = (f32[2,2,3,320,128]{4,3,2,1,0:T(8,128)S(1)}, f32[2,512,128]{2,1,0:T(8,128)S(1)}, f32[8,128]{1,0:T(8,128)S(1)}) custom-call(f32[2,2,3,320,128]{4,3,2,1,0:T(8,128)S(1)} %copy-done.10, f32[3,512,128]{2,1,0:T(8,128)S(1)} %get-tuple-element.21.sums, f32[8,128]{1,0:T(8,128)S(1)} %get-tuple-element.22.loss, ...), custom_call_target="tpu_custom_call" | custom-call | tf_op jit(solution)/shard_map/pallas_call | solution.py:586
  67.0 0.0 copy-start
  67.0 1.3 %copy-done = f32[2,2,3,320,128]{4,3,2,1,0:T(8,128)} copy-done((f32[2,2,3,320,128]{4,3,2,1,0:T(8,128)}, f32[2,2,3,320,128]{4,3,2,1,0:T(8,128)S(1)}, u32[]{:S(2)}) %copy-start) | copy-done | bytes 1966104
  68.3 0.0 copy-done.7
  68.3 0.0 copy-done.9
  68.3 12.7 %shard_map.124 = (f32[2,2,3,320,128]{4,3,2,1,0:T(8,128)}, f32[3,512,128]{2,1,0:T(8,128)S(1)}, f32[8,128]{1,0:T(8,128)S(1)}) custom-call(s32[2]{0:T(128)S(1)} %copy-done.13, s32[2]{0:T(128)S(1)} %copy-done.14, s32[2]{0:T(128)S(1)} %copy-done.15, f32[2,2,3,320,128]{4,3,2,1,0:T(8,128)} %copy-done, f32[2,512,128]{2,1,0:T(8,128)S(1)} %get-tuple-element.24.probe.old, ...), custom_call_target="tpu_custom_call" | custom-call | tf_op jit(solution)/shard_map/pallas_call | solution.py:191
  81.0 0.0 copy-start.3
  81.0 1.5 %copy-done.3 = f32[2,2,3,320,128]{4,3,2,1,0:T(8,128)S(1)} copy-done((f32[2,2,3,320,128]{4,3,2,1,0:T(8,128)S(1)}, f32[2,2,3,320,128]{4,3,2,1,0:T(8,128)}, u32[]{:S(2)}) %copy-start.3) | copy-done | bytes 1966104
  82.5 0.0 copy-start.1
  82.5 26.1 %shard_map.125 = (f32[2,2,3,64,128]{4,3,2,1,0:T(8,128)S(1)}, f32[2,2,3,64,128]{4,3,2,1,0:T(8,128)S(1)}, f32[2,512,128]{2,1,0:T(8,128)S(1)}, f32[8,128]{1,0:T(8,128)S(1)}) custom-call(f32[2,2,3,320,128]{4,3,2,1,0:T(8,128)S(1)} %copy-done.3, f32[3,512,128]{2,1,0:T(8,128)S(1)} %get-tuple-element.26.sums, f32[8,128]{1,0:T(8,128)S(1)} %get-tuple-element.27.loss, ...), custom_call_target="tpu_custom_call" | custom-call | tf_op jit(solution)/shard_map/pallas_call | solution.py:586
  108.6 0.0 copy-done.1
  108.6 0.0 copy-start.4
  108.6 1.5 %copy-done.4 = f32[2,2,3,320,128]{4,3,2,1,0:T(8,128)S(1)} copy-done((f32[2,2,3,320,128]{4,3,2,1,0:T(8,128)S(1)}, f32[2,2,3,320,128]{4,3,2,1,0:T(8,128)}, u32[]{:S(2)}) %copy-start.4) | copy-done | bytes 1966104
  110.1 1.6 %shard_map.126 = (f32[2,2,192,384]{3,2,1,0:T(8,128)}, f32[2,256,256]{2,1,0:T(8,128)}, f32[2]{0:T(128)}) custom-call(f32[2,2,3,320,128]{4,3,2,1,0:T(8,128)S(1)} %copy-done.1, f32[2,2,3,320,128]{4,3,2,1,0:T(8,128)S(1)} %copy-done.4, f32[2,2,3,64,128]{4,3,2,1,0:T(8,128)S(1)} %get-tuple-element.28.above, f32[2,2,3,64,128]{4,3,2,1,0:T(8,128)S(1)} %get-tuple-element.29.below, ...), custom_call_target="tpu_custom_call" | custom-call | tf_op jit(solution)/shard_map/pallas_call | solution.py:636
Async XLA Ops:
  0.6 15.4 %copy-start.5 = (bf16[1536,512]{1,0:T(8,128)(2,1)S(1)}, bf16[1536,512]{1,0:T(8,128)(2,1)}, u32[]{:S(2)}) copy-start(bf16[1536,512]{1,0:T(8,128)(2,1)} %constant.9.clone.dft_r) | copy-start | bytes 4718596
  0.6 1.4 %copy-start.11 = (f32[2,2,192,384]{3,2,1,0:T(8,128)S(1)}, f32[2,2,192,384]{3,2,1,0:T(8,128)}, u32[]{:S(2)}) copy-start(f32[2,2,192,384]{3,2,1,0:T(8,128)} %own.1) | copy-start | bytes 3538948
  2.0 1.0 copy-start.12
  3.1 12.9 %copy-start.13 = (s32[2]{0:T(128)S(1)}, s32[2]{0:T(128)}, u32[]{:S(2)}) copy-start(s32[2]{0:T(128)} %rows_ref.3) | copy-start | bytes 28
  3.1 12.9 %copy-start.14 = (s32[2]{0:T(128)S(1)}, s32[2]{0:T(128)}, u32[]{:S(2)}) copy-start(s32[2]{0:T(128)} %cols_ref.3) | copy-start | bytes 28
  3.1 12.9 %copy-start.15 = (s32[2]{0:T(128)S(1)}, s32[2]{0:T(128)}, u32[]{:S(2)}) copy-start(s32[2]{0:T(128)} %first_ref.3) | copy-start | bytes 28
  14.7 1.3 %copy-start.2 = (f32[2,2,3,320,128]{4,3,2,1,0:T(8,128)}, f32[2,2,3,320,128]{4,3,2,1,0:T(8,128)S(1)}, u32[]{:S(2)}) copy-start(f32[2,2,3,320,128]{4,3,2,1,0:T(8,128)S(1)} %get-tuple-element.18.field.refs_0_) | copy-start | bytes 5898244
  16.0 1.4 %copy-start.6 = (bf16[512,1536]{1,0:T(8,128)(2,1)S(1)}, bf16[512,1536]{1,0:T(8,128)(2,1)}, u32[]{:S(2)}) copy-start(bf16[512,1536]{1,0:T(8,128)(2,1)} %constant.8.clone.dft_l) | copy-start | bytes 4718596
  17.4 1.0 copy-start.8
  31.1 1.5 %copy-start.10 = (f32[2,2,3,320,128]{4,3,2,1,0:T(8,128)S(1)}, f32[2,2,3,320,128]{4,3,2,1,0:T(8,128)}, u32[]{:S(2)}) copy-start(f32[2,2,3,320,128]{4,3,2,1,0:T(8,128)} %get-tuple-element.20.grad) | copy-start | bytes 5898244
  32.7 35.6 %copy-start.7 = (bf16[512,1536]{1,0:T(8,128)(2,1)S(1)}, bf16[512,1536]{1,0:T(8,128)(2,1)}, u32[]{:S(2)}) copy-start(bf16[512,1536]{1,0:T(8,128)(2,1)} %constant.8.clone.dft_l) | copy-start | bytes 4718596
  32.7 35.6 %copy-start.9 = (f32[2,256,256]{2,1,0:T(8,128)S(1)}, f32[2,256,256]{2,1,0:T(8,128)}, u32[]{:S(2)}) copy-start(f32[2,256,256]{2,1,0:T(8,128)} %intensity.3) | copy-start | bytes 1572868
  67.0 1.3 %copy-start = (f32[2,2,3,320,128]{4,3,2,1,0:T(8,128)}, f32[2,2,3,320,128]{4,3,2,1,0:T(8,128)S(1)}, u32[]{:S(2)}) copy-start(f32[2,2,3,320,128]{4,3,2,1,0:T(8,128)S(1)} %get-tuple-element.23.field) | copy-start | bytes 5898244
  81.0 1.5 %copy-start.3 = (f32[2,2,3,320,128]{4,3,2,1,0:T(8,128)S(1)}, f32[2,2,3,320,128]{4,3,2,1,0:T(8,128)}, u32[]{:S(2)}) copy-start(f32[2,2,3,320,128]{4,3,2,1,0:T(8,128)} %get-tuple-element.25.grad) | copy-start | bytes 5898244
  82.5 26.1 %copy-start.1 = (f32[2,2,3,320,128]{4,3,2,1,0:T(8,128)S(1)}, f32[2,2,3,320,128]{4,3,2,1,0:T(8,128)}, u32[]{:S(2)}) copy-start(f32[2,2,3,320,128]{4,3,2,1,0:T(8,128)} %copy-done) | copy-start | bytes 5898244
  108.6 1.5 %copy-start.4 = (f32[2,2,3,320,128]{4,3,2,1,0:T(8,128)S(1)}, f32[2,2,3,320,128]{4,3,2,1,0:T(8,128)}, u32[]{:S(2)}) copy-start(f32[2,2,3,320,128]{4,3,2,1,0:T(8,128)} %get-tuple-element.25.grad) | copy-start | bytes 5898244

commit v5 on v4

--- a/solution.py
+++ b/solution.py
@@ -19,7 +19,7 @@
 TINY = 1e-06
 LANES = 128
 STRIP = 32
-VMEM_LIMIT = 48 * 1024 * 1024
+VMEM_LIMIT = 24 * 1024 * 1024
 MESH = pl.DeviceIdType.MESH
 
 

time: 112 us -> 100 us (0.89)
  Pallas kernels: 98.9 us -> 91.5 us
  local copies, waits for them, and re-layouts: 12.1 us -> 7.73 us
    pallas_call x2, Pallas kernels: 25.4 us -> 19.3 us  [local_terms(): pl.pallas_call(local_kernel, out_shape=(jax.ShapeDtypeStruct(field.shape,...]
    unnamed x32 -> x28, local copies, waits for them, and re-layouts: 12.1 us -> 7.73 us
    pallas_call x2, Pallas kernels: 60.3 us -> 59 us  [renew(): pl.pallas_call(functools.partial(renew_kernel, devices, last), out_shape=...]
where the time goes in v5:
time: 100 us
  Pallas kernels  91.5 us (92%)
  local copies, waits for them, and re-layouts  7.73 us (8%)
    pallas_call x2, Pallas kernels, renew(): pl.pallas_call(functools.partial(renew_kernel, devices, last), out_shape=...  59 us
    pallas_call x2, Pallas kernels, local_terms(): pl.pallas_call(local_kernel, out_shape=(jax.ShapeDtypeStruct(field.shape,...  19.3 us
    pallas_call x1, Pallas kernels, first_field(): pl.pallas_call(functools.partial(first_kernel, lax.axis_size('row')), out...  11.6 us
    unnamed x28, local copies, waits for them, and re-layouts  7.73 us

profile of v5, /device:TPU:1, one launch (start us, length us, event | category | flops | bytes accessed | tf_op | source)
XLA Modules:
  0.0 100.2 jit_solution(11575814321119811135)
XLA Ops:
  0.6 0.0 copy-start
  0.6 0.0 copy-start.9
  0.7 1.4 %copy-done.9 = f32[2,2,192,384]{3,2,1,0:T(8,128)S(1)} copy-done((f32[2,2,192,384]{3,2,1,0:T(8,128)S(1)}, f32[2,2,192,384]{3,2,1,0:T(8,128)}, u32[]{:S(2)}) %copy-start.9) | copy-done | bytes 1179672
  2.0 0.0 copy-start.10
  2.0 1.0 %copy-done.10 = f32[2,256,256]{2,1,0:T(8,128)S(1)} copy-done((f32[2,256,256]{2,1,0:T(8,128)S(1)}, f32[2,256,256]{2,1,0:T(8,128)}, u32[]{:S(2)}) %copy-start.10) | copy-done | bytes 524312
  3.1 0.0 copy-start.11
  3.1 0.0 copy-start.12
  3.1 0.0 copy-start.13
  3.1 11.6 %shard_map.121 = (f32[2,2,3,320,128]{4,3,2,1,0:T(8,128)S(1)}, f32[2,512,128]{2,1,0:T(8,128)S(1)}) custom-call(f32[2,2,192,384]{3,2,1,0:T(8,128)S(1)} %copy-done.9, f32[2,256,256]{2,1,0:T(8,128)S(1)} %copy-done.10), custom_call_target="tpu_custom_call" | custom-call | tf_op jit(solution)/shard_map/pallas_call | solution.py:289
  14.7 0.0 copy-done
  14.7 0.0 copy-done.11
  14.7 0.0 copy-done.12
  14.7 0.0 copy-done.13
  14.7 0.0 copy-start.1
  14.7 1.4 %copy-done.1 = bf16[512,1536]{1,0:T(8,128)(2,1)S(1)} copy-done((bf16[512,1536]{1,0:T(8,128)(2,1)S(1)}, bf16[512,1536]{1,0:T(8,128)(2,1)}, u32[]{:S(2)}) %copy-start.1) | copy-done | bytes 1572888
  16.1 0.0 copy-start.3
  16.1 1.4 %copy-done.3 = bf16[1536,512]{1,0:T(8,128)(2,1)S(1)} copy-done((bf16[1536,512]{1,0:T(8,128)(2,1)S(1)}, bf16[1536,512]{1,0:T(8,128)(2,1)}, u32[]{:S(2)}) %copy-start.3) | copy-done | bytes 1572888
  17.6 0.0 copy-start.5
  17.6 1.4 %copy-done.5 = bf16[512,1536]{1,0:T(8,128)(2,1)S(1)} copy-done((bf16[512,1536]{1,0:T(8,128)(2,1)S(1)}, bf16[512,1536]{1,0:T(8,128)(2,1)}, u32[]{:S(2)}) %copy-start.5) | copy-done | bytes 1572888
  19.0 0.0 copy-start.7
  19.0 1.0 %copy-done.7 = f32[2,256,256]{2,1,0:T(8,128)S(1)} copy-done((f32[2,256,256]{2,1,0:T(8,128)S(1)}, f32[2,256,256]{2,1,0:T(8,128)}, u32[]{:S(2)}) %copy-start.7) | copy-done | bytes 524312
  20.0 9.6 %shard_map.122 = (f32[2,2,3,320,128]{4,3,2,1,0:T(8,128)S(1)}, f32[3,512,128]{2,1,0:T(8,128)S(1)}, f32[8,128]{1,0:T(8,128)S(1)}) custom-call(s32[2]{0:T(128)S(1)} %copy-done.11, s32[2]{0:T(128)S(1)} %copy-done.12, s32[2]{0:T(128)S(1)} %copy-done.13, f32[2,2,3,320,128]{4,3,2,1,0:T(8,128)S(1)} %get-tuple-element.18.field.refs_0_, ...), custom_call_target="tpu_custom_call" | custom-call | tf_op jit(solution)/shard_map/pallas_call | solution.py:191
  29.6 0.0 copy-start.2
  29.6 0.0 copy-start.4
  29.7 0.0 copy-start.6
  29.7 0.0 copy-start.8
  29.7 32.6 %shard_map.123 = (f32[2,2,3,320,128]{4,3,2,1,0:T(8,128)S(1)}, f32[2,512,128]{2,1,0:T(8,128)S(1)}, f32[8,128]{1,0:T(8,128)S(1)}) custom-call(f32[2,2,3,320,128]{4,3,2,1,0:T(8,128)S(1)} %get-tuple-element.20.grad, f32[3,512,128]{2,1,0:T(8,128)S(1)} %get-tuple-element.21.sums, f32[8,128]{1,0:T(8,128)S(1)} %get-tuple-element.22.loss, ...), custom_call_target="tpu_custom_call" | custom-call | tf_op jit(solution)/shard_map/pallas_call | solution.py:586
  62.3 0.0 copy-done.2
  62.3 0.0 copy-done.4
  62.3 0.0 copy-done.6
  62.3 0.0 copy-done.8
  62.3 9.7 %shard_map.124 = (f32[2,2,3,320,128]{4,3,2,1,0:T(8,128)S(1)}, f32[3,512,128]{2,1,0:T(8,128)S(1)}, f32[8,128]{1,0:T(8,128)S(1)}) custom-call(s32[2]{0:T(128)S(1)} %copy-done.11, s32[2]{0:T(128)S(1)} %copy-done.12, s32[2]{0:T(128)S(1)} %copy-done.13, f32[2,2,3,320,128]{4,3,2,1,0:T(8,128)S(1)} %get-tuple-element.23.field, ...), custom_call_target="tpu_custom_call" | custom-call | tf_op jit(solution)/shard_map/pallas_call | solution.py:191
  72.0 26.4 %shard_map.125 = (f32[2,2,3,64,128]{4,3,2,1,0:T(8,128)S(1)}, f32[2,2,3,64,128]{4,3,2,1,0:T(8,128)S(1)}, f32[2,512,128]{2,1,0:T(8,128)S(1)}, f32[8,128]{1,0:T(8,128)S(1)}) custom-call(f32[2,2,3,320,128]{4,3,2,1,0:T(8,128)S(1)} %get-tuple-element.25.grad, f32[3,512,128]{2,1,0:T(8,128)S(1)} %get-tuple-element.26.sums, f32[8,128]{1,0:T(8,128)S(1)} %get-tuple-element.27.loss, ...), custom_call_target="tpu_custom_call" | custom-call | tf_op jit(solution)/shard_map/pallas_call | solution.py:586
  98.4 1.6 %shard_map.126 = (f32[2,2,192,384]{3,2,1,0:T(8,128)}, f32[2,256,256]{2,1,0:T(8,128)}, f32[2]{0:T(128)}) custom-call(f32[2,2,3,320,128]{4,3,2,1,0:T(8,128)S(1)} %get-tuple-element.23.field, f32[2,2,3,320,128]{4,3,2,1,0:T(8,128)S(1)} %get-tuple-element.25.grad, f32[2,2,3,64,128]{4,3,2,1,0:T(8,128)S(1)} %get-tuple-element.28.above, ...), custom_call_target="tpu_custom_call" | custom-call | tf_op jit(solution)/shard_map/pallas_call | solution.py:636
Async XLA Ops:
  0.6 14.1 %copy-start = (bf16[1536,512]{1,0:T(8,128)(2,1)S(1)}, bf16[1536,512]{1,0:T(8,128)(2,1)}, u32[]{:S(2)}) copy-start(bf16[1536,512]{1,0:T(8,128)(2,1)} %constant.11.clone.spread_r) | copy-start | bytes 4718596
  0.6 1.4 %copy-start.9 = (f32[2,2,192,384]{3,2,1,0:T(8,128)S(1)}, f32[2,2,192,384]{3,2,1,0:T(8,128)}, u32[]{:S(2)}) copy-start(f32[2,2,192,384]{3,2,1,0:T(8,128)} %own.1) | copy-start | bytes 3538948
  2.0 1.0 %copy-start.10 = (f32[2,256,256]{2,1,0:T(8,128)S(1)}, f32[2,256,256]{2,1,0:T(8,128)}, u32[]{:S(2)}) copy-start(f32[2,256,256]{2,1,0:T(8,128)} %probe.1) | copy-start | bytes 1572868
  3.1 11.6 %copy-start.11 = (s32[2]{0:T(128)S(1)}, s32[2]{0:T(128)}, u32[]{:S(2)}) copy-start(s32[2]{0:T(128)} %rows_ref.3) | copy-start | bytes 28
  3.1 11.6 %copy-start.12 = (s32[2]{0:T(128)S(1)}, s32[2]{0:T(128)}, u32[]{:S(2)}) copy-start(s32[2]{0:T(128)} %cols_ref.3) | copy-start | bytes 28
  3.1 11.6 %copy-start.13 = (s32[2]{0:T(128)S(1)}, s32[2]{0:T(128)}, u32[]{:S(2)}) copy-start(s32[2]{0:T(128)} %first_ref.3) | copy-start | bytes 28
  14.7 1.4 %copy-start.1 = (bf16[512,1536]{1,0:T(8,128)(2,1)S(1)}, bf16[512,1536]{1,0:T(8,128)(2,1)}, u32[]{:S(2)}) copy-start(bf16[512,1536]{1,0:T(8,128)(2,1)} %constant.10.clone.spread_l) | copy-start | bytes 4718596
  16.1 1.4 %copy-start.3 = (bf16[1536,512]{1,0:T(8,128)(2,1)S(1)}, bf16[1536,512]{1,0:T(8,128)(2,1)}, u32[]{:S(2)}) copy-start(bf16[1536,512]{1,0:T(8,128)(2,1)} %constant.9.clone.dft_r) | copy-start | bytes 4718596
  17.6 1.4 %copy-start.5 = (bf16[512,1536]{1,0:T(8,128)(2,1)S(1)}, bf16[512,1536]{1,0:T(8,128)(2,1)}, u32[]{:S(2)}) copy-start(bf16[512,1536]{1,0:T(8,128)(2,1)} %constant.8.clone.dft_l) | copy-start | bytes 4718596
  19.0 1.0 %copy-start.7 = (f32[2,256,256]{2,1,0:T(8,128)S(1)}, f32[2,256,256]{2,1,0:T(8,128)}, u32[]{:S(2)}) copy-start(f32[2,256,256]{2,1,0:T(8,128)} %intensity.3) | copy-start | bytes 1572868
  29.6 32.7 %copy-start.2 = (bf16[512,1536]{1,0:T(8,128)(2,1)S(1)}, bf16[512,1536]{1,0:T(8,128)(2,1)}, u32[]{:S(2)}) copy-start(bf16[512,1536]{1,0:T(8,128)(2,1)} %constant.10.clone.spread_l) | copy-start | bytes 4718596
  29.6 32.7 %copy-start.4 = (bf16[1536,512]{1,0:T(8,128)(2,1)S(1)}, bf16[1536,512]{1,0:T(8,128)(2,1)}, u32[]{:S(2)}) copy-start(bf16[1536,512]{1,0:T(8,128)(2,1)} %constant.9.clone.dft_r) | copy-start | bytes 4718596
  29.7 32.6 %copy-start.6 = (bf16[512,1536]{1,0:T(8,128)(2,1)S(1)}, bf16[512,1536]{1,0:T(8,128)(2,1)}, u32[]{:S(2)}) copy-start(bf16[512,1536]{1,0:T(8,128)(2,1)} %constant.8.clone.dft_l) | copy-start | bytes 4718596
  29.7 32.6 %copy-start.8 = (f32[2,256,256]{2,1,0:T(8,128)S(1)}, f32[2,256,256]{2,1,0:T(8,128)}, u32[]{:S(2)}) copy-start(f32[2,256,256]{2,1,0:T(8,128)} %intensity.3) | copy-start | bytes 1572868
